TPU v7x, 512 devices: a whole 4x4x16 slice. The times are simulated.
512 devices in a mesh: grid: 128 (over x, z, core), rep: 4 (over y).
Axes of the slice: x: 4, y: 4, z: 16, core: 2. Of those that a mesh axis runs over, the one named last changes fastest.
Arguments:
- amplitudes: float32 [2048, 1440], P('grid'), may hold values from -6 to 6
- denominators: float32 [2048, 1440], P('grid'), may hold values from 0.5 to 5
- integrals: bfloat16 [737280, 1440], P(('grid', 'rep')), may hold values from -0.0390625 to 0.0390625
- amp_owner: int32 [65536, 1], P(('grid', 'rep')), may hold values from 0 to 127; in each aligned block of 128 rows (0 to 127, 128 to 255, ...) at most 2 rows name the same one
- amp_slot: int32 [65536], P(('grid', 'rep')), may hold values from 0 to 15
- res_owner: int32 [65536, 1], P(('grid', 'rep')), may hold values from 0 to 127; in each aligned block of 128 rows (0 to 127, 128 to 255, ...) at most 2 rows name the same one
- res_slot: int32 [65536], P(('grid', 'rep')), may hold values from 0 to 15
- task_count: int32 [512], P(('grid', 'rep')), may hold values from 1 to 128, 32768 in all
Outputs:
- residual: float32 [2048, 1440], P('grid')
- updated: float32 [2048, 1440], P('grid')
Inputs may be any that keep to these rules, and one draw needn't show every extreme that they name: `amp_owner`: among the 128 rows of one device, at most 2 name any one owner, and in some devices one owner is named exactly 2 times. `res_owner`: among the 128 rows of one device, at most 2 name any one owner, and in some devices one owner is named exactly 2 times. `task_count`: the counts over all devices sum to 128 * 4 * 64, and some device is full.
All inputs are finite; a program needn't handle non-finite values.
Results may differ from a plain program's by a relative error of at most 0.0029.
Values may be sent and summed in bfloat16 or wider, within the bound.
No kernel may reach another device: no remote copies, remote signals or barrier semaphores. Data moves between devices by JAX's collectives and lax.ppermute only.
A program may use at most 64 MiB of HBM per device.

v0:
```python
import jax
import jax.numpy as jnp
from jax import lax
from jax.sharding import PartitionSpec as P


def positions(owners, groups, capacity):
    onehot = (owners[:, None] == jnp.arange(groups, dtype=jnp.int32)[None, :]).astype(jnp.int32)
    before = jnp.cumsum(onehot, axis=0) - onehot
    ranking = jnp.sum(before * onehot, axis=1)
    return owners * capacity + ranking


def per_device(
    amplitudes, denominators, integrals, amp_owner, amp_slot, res_owner, res_slot, task_count
):
    groups = lax.axis_size("grid")
    task_total = amp_slot.shape[0]
    tile_total = amplitudes.shape[0]
    width = amplitudes.shape[1]
    capacity = max(2, 2 * task_total // groups)
    buffer_rows = groups * capacity
    active = jnp.arange(task_total, dtype=jnp.int32) < task_count[0]
    fetch_pos = positions(amp_owner[:, 0], groups, capacity)
    wanted_slots = (
        jnp.full((buffer_rows,), -1, jnp.int32).at[fetch_pos].set(jnp.where(active, amp_slot, -1))
    )
    wanted = lax.all_to_all(
        wanted_slots.reshape(groups, capacity), "grid", split_axis=0, concat_axis=0, tiled=True
    )
    valid = wanted >= 0
    found = amplitudes[jnp.clip(wanted, 0, tile_total - 1)].astype(jnp.bfloat16)
    found = jnp.where(valid[:, :, None], found, jnp.zeros_like(found))
    answered = lax.all_to_all(found, "grid", split_axis=0, concat_axis=0, tiled=True)
    fetched = answered.reshape(buffer_rows, width)[fetch_pos]
    contrib = jnp.dot(fetched, integrals, preferred_element_type=jnp.float32)
    contrib = jnp.where(active[:, None], contrib, jnp.zeros_like(contrib))
    send_pos = positions(res_owner[:, 0], groups, capacity)
    outgoing = (
        jnp.zeros((buffer_rows, width), jnp.float32)
        .at[send_pos]
        .set(contrib)
        .reshape(groups, capacity, width)
    )
    targets = (
        jnp.full((buffer_rows,), -1, jnp.int32).at[send_pos].set(jnp.where(active, res_slot, -1))
    )
    incoming, landed = (
        lax.all_to_all(outgoing, "grid", split_axis=0, concat_axis=0, tiled=True),
        lax.all_to_all(
            targets.reshape(groups, capacity), "grid", split_axis=0, concat_axis=0, tiled=True
        ),
    )
    picker = (
        landed.reshape(-1)[None, :] == jnp.arange(tile_total, dtype=jnp.int32)[:, None]
    ).astype(jnp.float32)
    partial_sum = jnp.dot(
        picker, incoming.reshape(buffer_rows, width), precision=lax.Precision.HIGHEST
    )
    residual = lax.psum(partial_sum, "rep")
    updated = amplitudes + residual / denominators
    return (residual, updated)


def solution(mesh):
    return jax.shard_map(
        per_device,
        mesh=mesh,
        in_specs=(
            P("grid", None),
            P("grid", None),
            P(("grid", "rep"), None),
            P(("grid", "rep"), None),
            P(("grid", "rep")),
            P(("grid", "rep"), None),
            P(("grid", "rep")),
            P(("grid", "rep")),
        ),
        out_specs=(P("grid", None), P("grid", None)),
        check_vma=False,
    )
```

profile of v0, /device:TPU:1, one launch (start us, length us, event | category | flops | bytes accessed | tf_op | source)
XLA Modules:
  0.0 272.3 jit_solution(7991181393870556209)
XLA Ops:
  7.2 0.0 copy-start
  7.9 0.7 fusion.2
  8.6 0.2 reduce_window_sum.18
  8.8 0.8 select_reduce_fusion
  9.6 0.7 fusion.7
  10.3 0.7 broadcast_select_fusion.1
  10.9 1.0 scatter_custom_fusion.1
  11.9 0.1 all_to_all.20
  12.1 35.2 %all_to_all.28 = s32[128,1,2]{2,1,0:T(1,128)S(1)} all-to-all(s32[128,1,2]{2,1,0:T(1,128)S(1)} %bitcast.29), channel_id=1, replica_groups=mesh['grid'=128,'rep'=4] {'grid'}, dimensions={0} | all-to-all | bytes 2048 | tf_op jit(solution)/shard_map/all_to_all | solution.py:28
  47.3 0.1 broadcast_compare_fusion
  47.4 0.1 copy.16
  47.5 0.1 broadcast_clamp_fusion
  47.6 0.1 reshape.63
  47.8 0.1 copy.17
  47.9 0.0 copy-done
  47.9 1.2 gather_fusion
  49.1 0.3 reshape.102
  49.5 0.0 copy-start.2
  49.5 1.7 broadcast_select_fusion
  51.1 6.6 %all-to-all-start.2 = ((bf16[128,2,1440]{2,1,0:T(2,128)(2,1)}), bf16[128,2,1440]{2,1,0:T(2,128)(2,1)S(1)}, u32[]{:S(2)}, u32[]{:S(2)}) async-start(bf16[128,2,1440]{2,1,0:T(2,128)(2,1)} %broadcast_select_fusion), calls=%async_computation.2 | async-start | bytes 1572864 | tf_op jit(solution)/shard_map/all_to_all | solution.py:34
  57.7 0.0 copy-done.2
  57.7 0.1 fusion.3
  57.8 0.2 reduce_window_sum.17
  58.0 0.2 select_reduce_fusion.1
  58.2 1.0 scatter_custom_fusion
  59.2 0.8 all_to_all.18
  59.9 41.4 %all-to-all-done.2 = bf16[128,2,1440]{2,1,0:T(2,128)(2,1)S(1)} async-done(((bf16[128,2,1440]{2,1,0:T(2,128)(2,1)}), bf16[128,2,1440]{2,1,0:T(2,128)(2,1)S(1)}, u32[]{:S(2)}, u32[]{:S(2)}) %all-to-all-start.2) | async-done | bytes 737312 | tf_op jit(solution)/shard_map/all_to_all | solution.py:34
  101.3 8.1 %all-to-all-start = ((s32[128,1,2]{2,1,0:T(1,128)}), s32[128,1,2]{2,1,0:T(1,128)S(1)}, u32[]{:S(2)}, u32[]{:S(2)}) async-start(s32[128,1,2]{2,1,0:T(1,128)} %bitcast.4), calls=%async_computation | async-start | bytes 131072 | tf_op jit(solution)/shard_map/all_to_all | solution.py:50
  109.4 0.6 reshape.58
  110.0 0.9 gather_fusion.1
  110.9 4.2 %convolution_select_fusion = f32[128,1440]{0,1:T(8,128)S(1)} fusion(bf16[128,1440]{1,0:T(8,128)(2,1)S(1)} %gather_fusion.1, bf16[1440,1440]{1,0:T(8,128)(2,1)} %param.10, pred[128]{0:T(512)(128)(4,1)S(1)} %iota_compare_fusion.4), kind=kOutput, calls=%fused_computation.5 | convolution fusion | flops 531025920 | bytes 5253248 | tf_op jit(solution)/shard_map/dot_general | solution.py:36
  115.1 0.3 copy.18
  115.3 1.5 scatter_custom_fusion.2
  116.8 2.1 reshape.59
  118.9 5.4 %all-to-all-done = s32[128,1,2]{2,1,0:T(1,128)S(1)} async-done(((s32[128,1,2]{2,1,0:T(1,128)}), s32[128,1,2]{2,1,0:T(1,128)S(1)}, u32[]{:S(2)}, u32[]{:S(2)}) %all-to-all-start) | async-done | bytes 1056 | tf_op jit(solution)/shard_map/all_to_all | solution.py:50
  124.4 10.8 %all-to-all-start.3 = ((f32[128,2,1440]{2,1,0:T(2,128)}), f32[128,2,1440]{2,1,0:T(2,128)S(1)}, u32[]{:S(2)}, u32[]{:S(2)}) async-start(f32[128,2,1440]{2,1,0:T(2,128)} %reshape.59), calls=%async_computation.3 | async-start | bytes 3145728 | tf_op jit(solution)/shard_map/all_to_all | solution.py:49
  135.1 0.0 all-reduce.2.cloned.1.call-start
  135.2 0.5 broadcast.102
  135.7 0.8 reduce.3
  136.5 0.1 eq.49
  136.7 75.3 %all-to-all-done.3 = f32[128,2,1440]{2,1,0:T(2,128)S(1)} async-done(((f32[128,2,1440]{2,1,0:T(2,128)}), f32[128,2,1440]{2,1,0:T(2,128)S(1)}, u32[]{:S(2)}, u32[]{:S(2)}) %all-to-all-start.3) | async-done | bytes 1474592 | tf_op jit(solution)/shard_map/all_to_all | solution.py:49
  211.9 1.1 reshape.60
  213.0 0.0 copy-start.1
  213.0 1.3 fusion.4
  214.3 0.0 all-reduce.2.cloned.1.call-update
  214.3 48.1 %all-reduce.2.cloned.1.call-done = f32[16,1440]{1,0:T(8,128)} async-done(((f32[16,1440]{1,0:T(8,128)}), f32[16,1440]{1,0:T(8,128)}) %all-reduce.2.cloned.1.call-update) | async-done | bytes 92176 | tf_op jit(solution)/shard_map/psum | solution.py:60
  262.4 1.6 divide_add_fusion
  263.9 1.5 copy.21
  (6 shorter events, 0.0 us)
Async XLA Ops:
  7.2 40.7 %copy-start = (f32[16,1440]{1,0:T(8,128)S(1)}, f32[16,1440]{1,0:T(8,128)}, u32[]{:S(2)}) copy-start(f32[16,1440]{1,0:T(8,128)} %param.8) | copy-start | bytes 276484
  49.5 8.3 %copy-start.2 = (s32[128,1]{0,1:T(1,128)S(1)}, s32[128,1]{0,1:T(1,128)}, u32[]{:S(2)}) copy-start(s32[128,1]{0,1:T(1,128)} %param.13) | copy-start | bytes 1540
  51.1 50.2 %all-to-all-start.2 = ((bf16[128,2,1440]{2,1,0:T(2,128)(2,1)}), bf16[128,2,1440]{2,1,0:T(2,128)(2,1)S(1)}, u32[]{:S(2)}, u32[]{:S(2)}) async-start(bf16[128,2,1440]{2,1,0:T(2,128)(2,1)} %broadcast_select_fusion), calls=%async_computation.2 | async-start | bytes 1572864 | tf_op jit(solution)/shard_map/all_to_all | solution.py:34
  101.3 23.1 %all-to-all-start = ((s32[128,1,2]{2,1,0:T(1,128)}), s32[128,1,2]{2,1,0:T(1,128)S(1)}, u32[]{:S(2)}, u32[]{:S(2)}) async-start(s32[128,1,2]{2,1,0:T(1,128)} %bitcast.4), calls=%async_computation | async-start | bytes 131072 | tf_op jit(solution)/shard_map/all_to_all | solution.py:50
  124.4 87.5 %all-to-all-start.3 = ((f32[128,2,1440]{2,1,0:T(2,128)}), f32[128,2,1440]{2,1,0:T(2,128)S(1)}, u32[]{:S(2)}, u32[]{:S(2)}) async-start(f32[128,2,1440]{2,1,0:T(2,128)} %reshape.59), calls=%async_computation.3 | async-start | bytes 3145728 | tf_op jit(solution)/shard_map/all_to_all | solution.py:49
  135.1 127.2 %all-reduce.2.cloned.1.call-start = ((), (), s32[]{:S(2)}) async-start(), calls=%async_computation.4 | async-start | bytes 196608 | tf_op jit(solution)/shard_map/psum | solution.py:60
  213.0 49.4 %copy-start.1 = (f32[16,1440]{1,0:T(8,128)S(1)}, f32[16,1440]{1,0:T(8,128)}, u32[]{:S(2)}) copy-start(f32[16,1440]{1,0:T(8,128)} %param.9) | copy-start | bytes 276484
Sparse Core Ops, SparseCore 0:
  214.4 47.9 all-reduce.1
where the time goes:
time: 274 us; the launch traced here: 272 us
  waiting for transfers between devices  170 us (62%)
  blocking collectives  35.2 us (13%)
  starting transfers between devices  25.4 us (9%)
  between operations  14.9 us (5%)
  local copies, waits for them, and re-layouts  13.4 us (5%)
  other arithmetic  7.74 us (3%)
  matrix products  5.43 us (2%)
    all_to_all x1, waiting for transfers between devices, per_device(): lax.all_to_all(outgoing, 'grid', split_axis=0, concat_axis=0, tiled=True)  75.3 us
    psum x1, waiting for transfers between devices, per_device(): residual = lax.psum(partial_sum, 'rep')  48.1 us
    all_to_all x1, waiting for transfers between devices, per_device(): lax.all_to_all(found, 'grid', split_axis=0, concat_axis=0, tiled=True)  41.4 us
    all_to_all x1, blocking collectives, per_device(): lax.all_to_all(wanted_slots.reshape(groups, capacity), 'grid', split_axis...  35.2 us
    all_to_all x1, starting transfers between devices, per_device(): lax.all_to_all(outgoing, 'grid', split_axis=0, concat_axis=0, tiled=True)  10.8 us
    all_to_all x1, starting transfers between devices, per_device(): lax.all_to_all(targets.reshape(groups, capacity), 'grid', split_axis=0, c...  8.08 us
    all_to_all x1, starting transfers between devices, per_device(): lax.all_to_all(found, 'grid', split_axis=0, concat_axis=0, tiled=True)  6.57 us
  transfers between devices with their start and end apart: 4, of which 4 were waited for; matrix products, arithmetic and copies ran while one was open for 5% of the time, Pallas kernels for 0%

commit v1 on v0

v1 whole, which is shorter than its diff:
```python
import jax
import jax.numpy as jnp
from jax import lax
from jax.experimental import pallas as pl
from jax.experimental.pallas import tpu as pltpu
from jax.sharding import Mesh, PartitionSpec as P

BF = jnp.bfloat16
F32 = jnp.float32
I32 = jnp.int32
TASKS = 128
PEERS = 64
CELLS = 256
WIDTH = 1440
BLOCK = ("x", "zl", "core", "rep")
RING = ("zh", "rep")


def iota(shape, dim):
    return lax.broadcasted_iota(I32, shape, dim)


def dot(a, b):
    return lax.dot_general(a, b, (((1,), (0,)), ((), ())), preferred_element_type=F32)


def cells(owner, rank):
    core = owner & 1
    zl = (owner >> 1) & 1
    zh = (owner >> 2) & 7
    x = owner >> 5
    peer = ((x * 2 + zl) * 2 + core) * 4 + (zh & 3)
    return peer * 4 + (zh >> 2) * 2 + rank


def place(owner_col):
    square = (TASKS, TASKS)
    row, col = iota(square, 0), iota(square, 1)
    owner_row = jnp.sum(jnp.where(row == col, owner_col, 0), axis=0, keepdims=True)
    same = owner_col == owner_row
    rank_col = jnp.sum(jnp.where(same & (col < row), 1, 0), axis=1, keepdims=True)
    rank_row = jnp.sum(jnp.where(same & (row < col), 1, 0), axis=0, keepdims=True)
    return cells(owner_col, rank_col), cells(owner_row, rank_row)


def to_col(row_vec):
    square = (TASKS, TASKS)
    return jnp.sum(jnp.where(iota(square, 0) == iota(square, 1), row_vec, 0), axis=1, keepdims=True)


def index_kernel(count_ref, ao_ref, as_ref, ro_ref, rs_ref, want_ref, gather_ref, scatter_ref):
    count = count_ref[0]
    live_col = iota((TASKS, 1), 0) < count
    live_row = iota((1, TASKS), 1) < count
    total = jnp.zeros((PEERS, 8), F32)
    for which, (o_ref, s_ref) in enumerate(((ao_ref, as_ref), (ro_ref, rs_ref))):
        col, row = place(o_ref[...])
        slot = to_col(s_ref[...])
        lane = iota((TASKS, 8), 1)
        value = jnp.where((lane == (col & 3) + 4 * which) & live_col, slot + 1, 0)
        peer = jnp.where(iota((PEERS, TASKS), 0) == (row >> 2), 1.0, 0.0)
        total = total + dot(peer.astype(BF), value.astype(F32).astype(BF))
        if which == 0:
            hit = (iota((TASKS, CELLS), 1) == col) & live_col
            gather_ref[...] = jnp.where(hit, 1.0, 0.0).astype(BF)
        else:
            hit = (iota((CELLS, TASKS), 0) == row) & live_row
            scatter_ref[...] = jnp.where(hit, 1.0, 0.0).astype(BF)
    want_ref[...] = total.astype(I32) - 1


def picks(want, half, first):
    spread = jnp.where(iota((CELLS, PEERS), 0) >> 2 == iota((CELLS, PEERS), 1), 1.0, 0.0)
    every = dot(spread.astype(BF), want.astype(F32).astype(BF)).astype(I32)
    cell = iota((CELLS, 8), 0)
    mine = iota((CELLS, 8), 1) == (cell & 3) + first
    slot = jnp.sum(jnp.where(mine, every, 0), axis=1, keepdims=True)
    part = (iota((CELLS, 1), 0) >> 1) & 1
    held = jnp.where(slot < 0, -1, jnp.bitwise_xor(part, half) * 16 + slot)
    return jnp.where(iota((CELLS, 32), 1) == held, 1.0, 0.0).astype(BF)


def answer_kernel(half_ref, want_ref, near_ref, far_ref, out_ref):
    rows = jnp.concatenate([near_ref[...], far_ref[...]], axis=0)
    out_ref[...] = dot(picks(want_ref[...], half_ref[0], 0), rows).astype(BF)


def task_kernel(gather_ref, rows_ref, scatter_ref, tile_ref, out_ref):
    operand = dot(gather_ref[...], rows_ref[...]).astype(BF)
    contrib = dot(operand, tile_ref[...]).astype(BF)
    out_ref[...] = dot(scatter_ref[...], contrib).astype(BF)


def collect_kernel(half_ref, want_ref, rows_ref, near_ref, far_ref):
    onehot = picks(want_ref[...], half_ref[0], 4)
    part = lax.dot_general(
        onehot, rows_ref[...], (((0,), (0,)), ((), ())), preferred_element_type=F32
    )
    near_ref[...] = part[:16].astype(BF)
    far_ref[...] = part[16:].astype(BF)


VM = pl.BlockSpec(memory_space=pltpu.VMEM)
SM = pl.BlockSpec(memory_space=pltpu.SMEM)


def call(kernel, ins, outs, *args, limit=16 << 20):
    shapes = tuple(jax.ShapeDtypeStruct(s, d) for s, d in outs)
    return pl.pallas_call(
        kernel,
        out_shape=shapes,
        in_specs=list(ins),
        out_specs=tuple(VM for _ in shapes),
        compiler_params=pltpu.CompilerParams(vmem_limit_bytes=limit),
    )(*args)


def spread_pairs(turn):
    pairs = []
    for zh in range(8):
        for y in range(4):
            pairs.append(((4 * ((zh // 4) ^ turn) + y) * 4 + zh % 4, zh * 4 + y))
    return pairs


def per_device(
    amplitudes, denominators, integrals, amp_owner, amp_slot, res_owner, res_slot, task_count
):
    half = (lax.axis_index("zh") // 4).astype(I32).reshape(1)
    low = amplitudes.astype(BF)
    near = lax.ppermute(low, RING, spread_pairs(0))
    far = lax.ppermute(low, RING, spread_pairs(1))
    want, gather, scatter = call(
        index_kernel,
        (SM, VM, VM, VM, VM),
        (((PEERS, 8), I32), ((TASKS, CELLS), BF), ((CELLS, TASKS), BF)),
        task_count,
        amp_owner,
        amp_slot.reshape(1, TASKS),
        res_owner,
        res_slot.reshape(1, TASKS),
    )
    wanted = lax.all_to_all(want.reshape(PEERS, 1, 8), BLOCK, 0, 0, tiled=True).reshape(PEERS, 8)
    (found,) = call(
        answer_kernel, (SM, VM, VM, VM), (((CELLS, WIDTH), BF),), half, wanted, near, far
    )
    fetched = lax.all_to_all(found.reshape(PEERS, 4, WIDTH), BLOCK, 0, 0, tiled=True)
    (sent,) = call(
        task_kernel,
        (VM, VM, VM, VM),
        (((CELLS, WIDTH), BF),),
        gather,
        fetched.reshape(CELLS, WIDTH),
        scatter,
        integrals,
        limit=32 << 20,
    )
    landed = lax.all_to_all(sent.reshape(PEERS, 4, WIDTH), BLOCK, 0, 0, tiled=True)
    part0, part1 = call(
        collect_kernel,
        (SM, VM, VM),
        (((16, WIDTH), BF), ((16, WIDTH), BF)),
        half,
        wanted,
        landed.reshape(CELLS, WIDTH),
    )
    back0 = lax.ppermute(part0, RING, [(d, s) for s, d in spread_pairs(0)])
    back1 = lax.ppermute(part1, RING, [(d, s) for s, d in spread_pairs(1)])
    mine = back0.astype(F32) + back1.astype(F32)
    copies = jnp.broadcast_to(mine[None], (4, 16, WIDTH))
    every = lax.all_to_all(copies, "rep", 0, 0, tiled=True)
    residual = jnp.sum(every, axis=0)
    return residual, amplitudes + residual / denominators


def solution(mesh):
    fine = Mesh(mesh.devices.reshape(4, 8, 2, 2, 4), ("x", "zh", "zl", "core", "rep"))
    grid = ("x", "zh", "zl", "core")
    every = grid + ("rep",)
    return jax.shard_map(
        per_device,
        mesh=fine,
        in_specs=(
            P(grid, None),
            P(grid, None),
            P(every, None),
            P(every, None),
            P(every),
            P(every, None),
            P(every),
            P(every),
        ),
        out_specs=(P(grid, None), P(grid, None)),
        check_vma=False,
    )
```

time: 274 us -> 117 us (0.43)
  the two profiles are of different devices: /device:TPU:1 before, /device:TPU:32 now
where the time goes in v1:
time: 117 us
  blocking collectives  53.2 us (45%)
  starting transfers between devices  31.2 us (27%)
  waiting for transfers between devices  19.8 us (17%)
  local copies, waits for them, and re-layouts  6.24 us (5%)
  Pallas kernels  3.35 us (3%)
  other arithmetic  1.6 us (1%)
  between operations  1.46 us (1%)
    all_to_all x1, blocking collectives, per_device(): lax.all_to_all(sent.reshape(PEERS, 4, WIDTH), BLOCK, 0, 0, tiled=True)  19.2 us
    all_to_all x1, blocking collectives, per_device(): lax.all_to_all(found.reshape(PEERS, 4, WIDTH), BLOCK, 0, 0, tiled=True)  18.7 us
    all_to_all x1, blocking collectives, per_device(): every = lax.all_to_all(copies, 'rep', 0, 0, tiled=True)  15.3 us
    ppermute x1, starting transfers between devices, per_device(): far = lax.ppermute(low, RING, spread_pairs(1))  14.8 us
    all_to_all x1, starting transfers between devices, per_device(): lax.all_to_all(want.reshape(PEERS, 1, 8), BLOCK, 0, 0, tiled=True)  13.2 us
    ppermute x1, waiting for transfers between devices, per_device(): back1 = lax.ppermute(part1, RING, [(d, s) for s, d in spread_pairs(1)])  12.8 us
    all_to_all x1, waiting for transfers between devices, per_device(): lax.all_to_all(want.reshape(PEERS, 1, 8), BLOCK, 0, 0, tiled=True)  7.08 us
    unnamed x14, local copies, waits for them, and re-layouts  5.1 us
  transfers between devices with their start and end apart: 5, of which 2 were waited for; matrix products, arithmetic and copies ran while one was open for 1% of the time, Pallas kernels for 1%

profile of v1, /device:TPU:32, one launch (start us, length us, event | category | flops | bytes accessed | tf_op | source)
XLA Modules:
  0.0 117.0 jit_solution(9456895246519769572)
XLA Ops:
  0.6 0.9 convert_element_type.9
  1.5 14.8 %collective-permute-start.1 = (bf16[16,1440]{1,0:T(8,128)(2,1)S(1)}, bf16[16,1440]{1,0:T(8,128)(2,1)S(1)}, u32[]{:S(2)}, u32[]{:S(2)}) collective-permute-start(bf16[16,1440]{1,0:T(8,128)(2,1)S(1)} %convert_element_type.9), channel_id=1, source_target_pairs={{64,0},{80,1},{96,2},{112,3},{65,16},{81,17},{97,18},{113,19},{66,... | collective-permute-start | bytes 138248 | tf_op jit(solution)/shard_map/ppermute | solution.py:132
  16.4 0.7 collective-permute-start
  17.7 0.8 copy.17.ao_ref
  18.4 0.8 copy.18.ro_ref
  19.2 0.0 copy-start.1
  19.2 0.6 copy-done.1
  19.9 0.0 copy-start.2
  19.9 0.7 copy-done.2
  20.5 1.2 %shard_map.95 = (s32[64,8]{1,0:T(8,128)}, bf16[128,256]{1,0:T(8,128)(2,1)S(1)}, bf16[256,128]{1,0:T(8,128)(2,1)S(1)}) custom-call(s32[1]{0:T(128)S(6)} %copy.20.count_ref, s32[128,1]{1,0:T(8,128)S(1)} %copy.17.ao_ref, s32[1,128]{1,0:T(1,128)S(1)} %bitcast.9, s32[128,1]{1,0:T(8,128)S(1)} %copy.18.ro_ref, s32[1,128]{1,0:T(1,128)S(1)} %bitcast.10), custom_call_target="tpu_custom_call" | custom-call | tf_op jit(solution)/shard_map/pallas_call | solution.py:109
  21.7 13.2 %all-to-all-start = ((s32[64,1,8]{2,1,0:T(1,128)}), s32[64,1,8]{2,1,0:T(1,128)S(1)}, u32[]{:S(2)}, u32[]{:S(2)}) async-start(s32[64,1,8]{2,1,0:T(1,128)} %bitcast.4), calls=%async_computation | async-start | bytes 65536 | tf_op jit(solution)/shard_map/all_to_all | solution.py:143
  34.9 7.1 %all-to-all-done = s32[64,1,8]{2,1,0:T(1,128)S(1)} async-done(((s32[64,1,8]{2,1,0:T(1,128)}), s32[64,1,8]{2,1,0:T(1,128)S(1)}, u32[]{:S(2)}, u32[]{:S(2)}) %all-to-all-start) | async-done | bytes 2080 | tf_op jit(solution)/shard_map/all_to_all | solution.py:143
  42.0 0.0 collective-permute-done.1.far_ref
  42.0 0.0 collective-permute-done.near_ref
  42.0 0.5 shard_map.96
  42.5 0.2 reshape.37
  42.7 18.7 %all_to_all.20 = bf16[64,4,1440]{2,1,0:T(4,128)(2,1)S(1)} all-to-all(bf16[64,4,1440]{2,1,0:T(4,128)(2,1)S(1)} %reshape.37), channel_id=1, replica_groups=mesh['x'=4,'zh'=8,'zl'=2,'core'=2,'rep'=4] {'x','zl','core','rep'}, dimensions={0} | all-to-all | bytes 1474560 | tf_op jit(solution)/shard_map/all_to_all | solution.py:147
  61.5 0.4 reshape.38.rows_ref
  61.8 0.0 copy-start
  61.8 2.2 %copy-done = bf16[1440,1440]{1,0:T(8,128)(2,1)S(1)} copy-done((bf16[1440,1440]{1,0:T(8,128)(2,1)S(1)}, bf16[1440,1440]{1,0:T(8,128)(2,1)}, u32[]{:S(2)}) %copy-start) | copy-done | bytes 4147224
  64.1 1.1 shard_map.97
  65.2 0.0 copy-start.3
  65.2 0.0 copy-start.5
  65.2 0.2 reshape.39
  65.4 19.2 %all_to_all.21 = bf16[64,4,1440]{2,1,0:T(4,128)(2,1)S(1)} all-to-all(bf16[64,4,1440]{2,1,0:T(4,128)(2,1)S(1)} %reshape.39), channel_id=1, replica_groups=mesh['x'=4,'zh'=8,'zl'=2,'core'=2,'rep'=4] {'x','zl','core','rep'}, dimensions={0} | all-to-all | bytes 1474560 | tf_op jit(solution)/shard_map/all_to_all | solution.py:158
  84.6 0.4 reshape.40.rows_ref
  85.0 0.5 shard_map.98
  85.5 0.7 collective-permute-start.2
  86.2 1.9 %collective-permute-start.3 = (bf16[16,1440]{1,0:T(8,128)(2,1)S(1)}, bf16[16,1440]{1,0:T(8,128)(2,1)S(1)}, u32[]{:S(2)}, u32[]{:S(2)}) collective-permute-start(bf16[16,1440]{1,0:T(8,128)(2,1)S(1)} %get-tuple-element.11), channel_id=1, source_target_pairs={{0,64},{1,80},{2,96},{3,112},{16,65},{17,81},{18,97},{19,113},{32,... | collective-permute-start | bytes 138248 | tf_op jit(solution)/shard_map/ppermute | solution.py:168
  88.1 0.0 collective-permute-done.2
  88.1 12.8 %collective-permute-done.3 = bf16[16,1440]{1,0:T(8,128)(2,1)S(1)} collective-permute-done((bf16[16,1440]{1,0:T(8,128)(2,1)S(1)}, bf16[16,1440]{1,0:T(8,128)(2,1)S(1)}, u32[]{:S(2)}, u32[]{:S(2)}) %collective-permute-start.3) | collective-permute-done | bytes 46112 | tf_op jit(solution)/shard_map/ppermute | solution.py:168
  101.0 15.3 %all_to_all.22 = f32[4,16,1440]{2,1,0:T(8,128)S(1)} all-to-all(f32[4,16,1440]{2,1,0:T(8,128)S(1)} %broadcast_in_dim.2), channel_id=1, replica_groups=mesh['x'=4,'zh'=8,'zl'=2,'core'=2,'rep'=4] {'rep'}, dimensions={0} | all-to-all | bytes 737280 | tf_op jit(solution)/shard_map/all_to_all | solution.py:171
  116.3 0.0 copy-done.3
  116.3 0.0 copy-done.5
  116.3 0.0 copy-start.4
  116.3 0.7 divide_add_fusion
  117.0 0.0 copy-done.4
  (3 shorter events, 0.1 us)
Async XLA Ops:
  1.5 40.4 %collective-permute-start.1 = (bf16[16,1440]{1,0:T(8,128)(2,1)S(1)}, bf16[16,1440]{1,0:T(8,128)(2,1)S(1)}, u32[]{:S(2)}, u32[]{:S(2)}) collective-permute-start(bf16[16,1440]{1,0:T(8,128)(2,1)S(1)} %convert_element_type.9), channel_id=1, source_target_pairs={{64,0},{80,1},{96,2},{112,3},{65,16},{81,17},{97,18},{113,19},{66,... | collective-permute-start | bytes 138248 | tf_op jit(solution)/shard_map/ppermute | solution.py:132
  16.4 25.6 %collective-permute-start = (bf16[16,1440]{1,0:T(8,128)(2,1)S(1)}, bf16[16,1440]{1,0:T(8,128)(2,1)S(1)}, u32[]{:S(2)}, u32[]{:S(2)}) collective-permute-start(bf16[16,1440]{1,0:T(8,128)(2,1)S(1)} %convert_element_type.9), channel_id=1, source_target_pairs={{0,0},{16,1},{32,2},{48,3},{1,16},{17,17},{33,18},{49,19},{2,32},{... | collective-permute-start | bytes 138248 | tf_op jit(solution)/shard_map/ppermute | solution.py:131
  19.2 0.7 copy-start.1
  19.9 0.7 copy-start.2
  21.7 20.3 %all-to-all-start = ((s32[64,1,8]{2,1,0:T(1,128)}), s32[64,1,8]{2,1,0:T(1,128)S(1)}, u32[]{:S(2)}, u32[]{:S(2)}) async-start(s32[64,1,8]{2,1,0:T(1,128)} %bitcast.4), calls=%async_computation | async-start | bytes 65536 | tf_op jit(solution)/shard_map/all_to_all | solution.py:143
  61.8 2.3 %copy-start = (bf16[1440,1440]{1,0:T(8,128)(2,1)S(1)}, bf16[1440,1440]{1,0:T(8,128)(2,1)}, u32[]{:S(2)}) copy-start(bf16[1440,1440]{1,0:T(8,128)(2,1)} %tile_ref.1) | copy-start | bytes 12441604
  65.2 51.1 %copy-start.3 = (f32[16,1440]{1,0:T(8,128)S(1)}, f32[16,1440]{1,0:T(8,128)}, u32[]{:S(2)}) copy-start(f32[16,1440]{1,0:T(8,128)} %param.8) | copy-start | bytes 276484
  65.2 51.1 %copy-start.5 = (f32[16,1440]{1,0:T(8,128)S(1)}, f32[16,1440]{1,0:T(8,128)}, u32[]{:S(2)}) copy-start(f32[16,1440]{1,0:T(8,128)} %param.9) | copy-start | bytes 276484
  85.5 2.6 %collective-permute-start.2 = (bf16[16,1440]{1,0:T(8,128)(2,1)S(1)}, bf16[16,1440]{1,0:T(8,128)(2,1)S(1)}, u32[]{:S(2)}, u32[]{:S(2)}) collective-permute-start(bf16[16,1440]{1,0:T(8,128)(2,1)S(1)} %get-tuple-element.10), channel_id=1, source_target_pairs={{0,0},{1,16},{2,32},{3,48},{16,1},{17,17},{18,33},{19,49},{32,2},{... | collective-permute-start | bytes 138248 | tf_op jit(solution)/shard_map/ppermute | solution.py:167
  86.2 14.7 %collective-permute-start.3 = (bf16[16,1440]{1,0:T(8,128)(2,1)S(1)}, bf16[16,1440]{1,0:T(8,128)(2,1)S(1)}, u32[]{:S(2)}, u32[]{:S(2)}) collective-permute-start(bf16[16,1440]{1,0:T(8,128)(2,1)S(1)} %get-tuple-element.11), channel_id=1, source_target_pairs={{0,64},{1,80},{2,96},{3,112},{16,65},{17,81},{18,97},{19,113},{32,... | collective-permute-start | bytes 138248 | tf_op jit(solution)/shard_map/ppermute | solution.py:168
  116.3 0.7 copy-start.4

commit v2 on v1

v2 whole, which is shorter than its diff:
```python
import jax
import jax.numpy as jnp
from jax import lax
from jax.experimental import pallas as pl
from jax.experimental.pallas import tpu as pltpu
from jax.sharding import Mesh, PartitionSpec as P

BF = jnp.bfloat16
F32 = jnp.float32
I32 = jnp.int32
TASKS = 128
PEERS = 64
CELLS = 256
WIDTH = 1440
SWAPS = (True, True)
CHUNKS = ((0, 384), (384, 384), (768, 384), (1152, 288))
BLOCK = ("x", "zl", "core", "rep")
RING = ("zh", "rep")


def iota(shape, dim):
    return lax.broadcasted_iota(I32, shape, dim)


def dot(a, b):
    return lax.dot_general(a, b, (((1,), (0,)), ((), ())), preferred_element_type=F32)


def cells(owner, rank, swap):
    core = owner & 1
    zl = (owner >> 1) & 1
    zh = (owner >> 2) & 7
    x = owner >> 5
    first, second = (zh >> 2, core) if swap else (core, zh >> 2)
    peer = ((x * 2 + zl) * 2 + first) * 4 + (zh & 3)
    return peer * 4 + second * 2 + rank


def place(owner_col, owner_row, swap):
    square = (TASKS, TASKS)
    row, col = iota(square, 0), iota(square, 1)
    same = owner_col == owner_row
    rank_col = jnp.sum(jnp.where(same & (col < row), 1, 0), axis=1, keepdims=True)
    rank_row = jnp.sum(jnp.where(same & (row < col), 1, 0), axis=0, keepdims=True)
    return cells(owner_col, rank_col, swap), cells(owner_row, rank_row, swap)


def to_col(row_vec):
    square = (TASKS, TASKS)
    return jnp.sum(jnp.where(iota(square, 0) == iota(square, 1), row_vec, 0), axis=1, keepdims=True)


def index_kernel(
    count_ref, ao_hbm, as_hbm, ro_hbm, rs_hbm, want_ref, gather_ref, scatter_ref,
    ao_ref, as_ref, ro_ref, rs_ref, sems,
):
    moves = [
        pltpu.make_async_copy(src, dst, sems.at[i])
        for i, (src, dst) in enumerate(
            ((ao_hbm, ao_ref), (as_hbm, as_ref), (ro_hbm, ro_ref), (rs_hbm, rs_ref))
        )
    ]
    for move in moves:
        move.start()
    for move in moves:
        move.wait()
    count = count_ref[0]
    live_col = iota((TASKS, 1), 0) < count
    live_row = iota((1, TASKS), 1) < count
    total = jnp.zeros((PEERS, 8), F32)
    for which, (o_ref, s_ref) in enumerate(((ao_ref, as_ref), (ro_ref, rs_ref))):
        owner = o_ref[...]
        col, row = place(to_col(owner), owner, SWAPS[which])
        slot = to_col(s_ref[...])
        lane = iota((TASKS, 8), 1)
        value = jnp.where((lane == (col & 3) + 4 * which) & live_col, slot + 1, 0)
        peer = jnp.where(iota((PEERS, TASKS), 0) == (row >> 2), 1.0, 0.0)
        total = total + dot(peer.astype(BF), value.astype(F32).astype(BF))
        if which == 0:
            hit = (iota((TASKS, CELLS), 1) == col) & live_col
            gather_ref[...] = jnp.where(hit, 1.0, 0.0).astype(BF)
        else:
            hit = (iota((CELLS, TASKS), 0) == row) & live_row
            scatter_ref[...] = jnp.where(hit, 1.0, 0.0).astype(BF)
    want_ref[...] = total.astype(I32) - 1


def picks(want, half, first):
    spread = jnp.where(iota((CELLS, PEERS), 0) >> 2 == iota((CELLS, PEERS), 1), 1.0, 0.0)
    every = dot(spread.astype(BF), want.astype(F32).astype(BF)).astype(I32)
    cell = iota((CELLS, 8), 0)
    mine = iota((CELLS, 8), 1) == (cell & 3) + first
    slot = jnp.sum(jnp.where(mine, every, 0), axis=1, keepdims=True)
    part = (iota((CELLS, 1), 0) >> 1) & 1
    held = jnp.where(slot < 0, -1, jnp.bitwise_xor(part, half) * 16 + slot)
    return jnp.where(iota((CELLS, 32), 1) == held, 1.0, 0.0).astype(BF)


def answer_kernel(half_ref, want_ref, rows_ref, out_ref):
    out_ref[...] = dot(picks(want_ref[...], half_ref[0], 0), rows_ref[...]).astype(BF)


def task_kernel(gather_ref, rows_ref, scatter_ref, tile_hbm, out_ref, tile_ref, sems):
    loads = [
        pltpu.make_async_copy(tile_hbm.at[pl.ds(k, n)], tile_ref.at[pl.ds(k, n)], sems.at[i])
        for i, (k, n) in enumerate(CHUNKS)
    ]
    for load in loads:
        load.start()
    operand = dot(gather_ref[...], rows_ref[...]).astype(BF)
    total = jnp.zeros((TASKS, WIDTH), F32)
    for load, (k, n) in zip(loads, CHUNKS):
        load.wait()
        total = total + dot(operand[:, k : k + n], tile_ref[k : k + n, :])
    out_ref[...] = dot(scatter_ref[...], total.astype(BF)).astype(BF)


def collect_kernel(want_ref, rows_ref, out_ref):
    onehot = picks(want_ref[...], 0, 4)
    part = lax.dot_general(
        onehot, rows_ref[...], (((0,), (0,)), ((), ())), preferred_element_type=F32
    )
    out_ref[...] = part.astype(BF)


VM = pl.BlockSpec(memory_space=pltpu.VMEM)
SM = pl.BlockSpec(memory_space=pltpu.SMEM)
HB = pl.BlockSpec(memory_space=pl.ANY)


def call(kernel, ins, outs, *args, scratch=(), limit=None):
    shapes = tuple(jax.ShapeDtypeStruct(s, d) for s, d in outs)
    return pl.pallas_call(
        kernel,
        out_shape=shapes,
        in_specs=list(ins),
        out_specs=tuple(VM for _ in shapes),
        scratch_shapes=list(scratch),
        compiler_params=pltpu.CompilerParams(vmem_limit_bytes=limit),
    )(*args)


def spread_pairs(turn):
    pairs = []
    for zh in range(8):
        for y in range(4):
            pairs.append(((4 * ((zh // 4) ^ turn) + y) * 4 + zh % 4, zh * 4 + y))
    return pairs


def return_pairs():
    pairs = []
    for a in range(2):
        for b in range(4):
            for k in range(2):
                for y in range(4):
                    pairs.append((((4 * a + b) * 2 + k) * 4 + y, ((4 * k + y) * 2 + a) * 4 + b))
    return pairs


def per_device(
    amplitudes, denominators, integrals, amp_owner, amp_slot, res_owner, res_slot, task_count
):
    half = (lax.axis_index("zh") // 4).astype(I32).reshape(1)
    other = lax.optimization_barrier(lax.ppermute(amplitudes, "core", ((0, 1), (1, 0))))
    pair = jnp.concatenate([amplitudes.astype(BF), other.astype(BF)])
    want, gather, scatter = call(
        index_kernel,
        (SM, HB, HB, HB, HB),
        (((PEERS, 8), I32), ((TASKS, CELLS), BF), ((CELLS, TASKS), BF)),
        task_count,
        amp_owner.reshape(1, TASKS),
        amp_slot.reshape(1, TASKS),
        res_owner.reshape(1, TASKS),
        res_slot.reshape(1, TASKS),
        scratch=[pltpu.VMEM((1, TASKS), I32)] * 4 + [pltpu.SemaphoreType.DMA((4,))],
    )
    pair, want = lax.optimization_barrier((pair, want))
    held = lax.ppermute(pair, ("zh", "core", "rep"), [(d, s) for s, d in return_pairs()])
    wanted = lax.all_to_all(want.reshape(PEERS, 1, 8), BLOCK, 0, 0, tiled=True).reshape(PEERS, 8)
    (found,) = call(
        answer_kernel, (SM, VM, VM), (((CELLS, WIDTH), BF),), half, wanted, held,
        limit=16 << 20,
    )
    fetched = lax.all_to_all(found.reshape(PEERS, 4, WIDTH), BLOCK, 0, 0, tiled=True)
    (sent,) = call(
        task_kernel,
        (VM, VM, VM, HB),
        (((CELLS, WIDTH), BF),),
        gather,
        fetched.reshape(CELLS, WIDTH),
        scatter,
        integrals,
        scratch=[pltpu.VMEM((WIDTH, WIDTH), BF), pltpu.SemaphoreType.DMA((len(CHUNKS),))],
        limit=50 << 20,
    )
    landed = lax.all_to_all(sent.reshape(PEERS, 4, WIDTH), BLOCK, 0, 0, tiled=True)
    (part,) = call(
        collect_kernel,
        (VM, VM),
        (((32, WIDTH), BF),),
        wanted,
        landed.reshape(CELLS, WIDTH),
        limit=16 << 20,
    )
    back = lax.ppermute(part, ("zh", "core", "rep"), return_pairs())
    copies = jnp.broadcast_to(back.reshape(2, 1, 16, WIDTH), (2, 4, 16, WIDTH))
    every = lax.all_to_all(copies.reshape(8, 16, WIDTH), ("core", "rep"), 0, 0, tiled=True)
    residual = jnp.sum(every.astype(F32), axis=0)
    return residual, amplitudes + residual / denominators


def solution(mesh):
    fine = Mesh(mesh.devices.reshape(4, 8, 2, 2, 4), ("x", "zh", "zl", "core", "rep"))
    grid = ("x", "zh", "zl", "core")
    every = grid + ("rep",)
    return jax.shard_map(
        per_device,
        mesh=fine,
        in_specs=(
            P(grid, None),
            P(grid, None),
            P(every, None),
            P(every, None),
            P(every),
            P(every, None),
            P(every),
            P(every),
        ),
        out_specs=(P(grid, None), P(grid, None)),
        check_vma=False,
    )
```

time: 117 us -> 109 us (0.932)
  the two profiles are of different devices: /device:TPU:32 before, /device:TPU:1 now
where the time goes in v2:
time: 109 us
  blocking collectives  50.8 us (47%)
  starting transfers between devices  32.6 us (30%)
  waiting for transfers between devices  15.2 us (14%)
  Pallas kernels  5.91 us (5%)
  other arithmetic  1.63 us (1%)
  between operations  1.47 us (1%)
  local copies, waits for them, and re-layouts  1.17 us (1%)
    all_to_all x1, blocking collectives, per_device(): lax.all_to_all(sent.reshape(PEERS, 4, WIDTH), BLOCK, 0, 0, tiled=True)  19.2 us
    all_to_all x1, blocking collectives, per_device(): lax.all_to_all(found.reshape(PEERS, 4, WIDTH), BLOCK, 0, 0, tiled=True)  18.8 us
    all_to_all x1, blocking collectives, per_device(): lax.all_to_all(copies.reshape(8, 16, WIDTH), ('core', 'rep'), 0, 0, tiled...  12.8 us
    ppermute x1, starting transfers between devices, per_device(): lax.ppermute(pair, ('zh', 'core', 'rep'), [(d, s) for s, d in return_pair...  9.97 us
    ppermute x1, starting transfers between devices, per_device(): lax.ppermute(amplitudes, 'core', ((0, 1), (1, 0)))  8.77 us
    ppermute x1, starting transfers between devices, per_device(): back = lax.ppermute(part, ('zh', 'core', 'rep'), return_pairs())  8.46 us
    all_to_all x1, waiting for transfers between devices, per_device(): lax.all_to_all(want.reshape(PEERS, 1, 8), BLOCK, 0, 0, tiled=True)  7.76 us
    ppermute x1, waiting for transfers between devices, per_device(): back = lax.ppermute(part, ('zh', 'core', 'rep'), return_pairs())  7.45 us
  transfers between devices with their start and end apart: 4, of which 2 were waited for; matrix products, arithmetic and copies ran while one was open for 0% of the time, Pallas kernels for 2%

profile of v2, /device:TPU:1, one launch (start us, length us, event | category | flops | bytes accessed | tf_op | source)
XLA Modules:
  0.0 108.8 jit_solution(3640800655606547803)
XLA Ops:
  0.6 0.9 convert_element_type.14
  1.5 8.8 %collective-permute-start = (bf16[16,1440]{1,0:T(8,128)(2,1)S(1)}, bf16[16,1440]{1,0:T(8,128)(2,1)S(1)}, u32[]{:S(2)}, u32[]{:S(2)}) collective-permute-start(bf16[16,1440]{1,0:T(8,128)(2,1)S(1)} %convert_element_type.14), channel_id=1, source_target_pairs={{0,4},{4,0},{1,5},{5,1},{2,6},{6,2},{3,7},{7,3},{8,12},{12,8},{9,1... | collective-permute-start | bytes 138248 | tf_op jit(solution)/shard_map/ppermute | solution.py:165
  11.0 1.8 %shard_map.95 = (s32[64,8]{1,0:T(8,128)}, bf16[128,256]{1,0:T(8,128)(2,1)}, bf16[256,128]{1,0:T(8,128)(2,1)}) custom-call(s32[1]{0:T(128)S(6)} %copy.12.count_ref, s32[1,128]{1,0:T(1,128)} %bitcast.16, s32[1,128]{1,0:T(1,128)} %bitcast.17, s32[1,128]{1,0:T(1,128)} %bitcast.18, s32[1,128]{1,0:T(1,128)} %bitcast.19), custom_call_target="tpu_custom_call" | custom-call | tf_op jit(solution)/shard_map/pallas_call | solution.py:133
  12.8 0.0 copy-start
  12.8 0.0 copy-start.1
  12.8 0.0 collective-permute-done
  12.8 10.0 %collective-permute-start.1 = (bf16[32,1440]{1,0:T(8,128)(2,1)S(1)}, bf16[32,1440]{1,0:T(8,128)(2,1)S(1)}, u32[]{:S(2)}, u32[]{:S(2)}) collective-permute-start(bf16[32,1440]{1,0:T(8,128)(2,1)S(1)} %pad_maximum_fusion), channel_id=1, source_target_pairs={{0,0},{16,1},{32,2},{48,3},{64,4},{80,5},{96,6},{112,7},{1,16},{17... | collective-permute-start | bytes 276488 | tf_op jit(solution)/shard_map/ppermute | solution.py:179
  22.8 5.4 %all-to-all-start = ((s32[64,1,8]{2,1,0:T(1,128)}), s32[64,1,8]{2,1,0:T(1,128)S(1)}, u32[]{:S(2)}, u32[]{:S(2)}) async-start(s32[64,1,8]{2,1,0:T(1,128)} %bitcast.15), calls=%async_computation | async-start | bytes 65536 | tf_op jit(solution)/shard_map/all_to_all | solution.py:180
  28.3 7.8 %all-to-all-done = s32[64,1,8]{2,1,0:T(1,128)S(1)} async-done(((s32[64,1,8]{2,1,0:T(1,128)}), s32[64,1,8]{2,1,0:T(1,128)S(1)}, u32[]{:S(2)}, u32[]{:S(2)}) %all-to-all-start) | async-done | bytes 2080 | tf_op jit(solution)/shard_map/all_to_all | solution.py:180
  36.0 0.0 collective-permute-done.1.rows_ref
  36.0 0.5 shard_map.96
  36.6 0.2 reshape.49
  36.8 18.8 %all_to_all.20 = bf16[64,4,1440]{2,1,0:T(4,128)(2,1)S(1)} all-to-all(bf16[64,4,1440]{2,1,0:T(4,128)(2,1)S(1)} %reshape.49), channel_id=1, replica_groups=mesh['x'=4,'zh'=8,'zl'=2,'core'=2,'rep'=4] {'x','zl','core','rep'}, dimensions={0} | all-to-all | bytes 1474560 | tf_op jit(solution)/shard_map/all_to_all | solution.py:185
  55.5 0.4 reshape.50.rows_ref
  55.9 0.0 copy-done
  55.9 0.0 copy-done.1
  55.9 3.0 %shard_map.97 = bf16[256,1440]{1,0:T(8,128)(2,1)S(1)} custom-call(bf16[128,256]{1,0:T(8,128)(2,1)S(1)} %copy-done, bf16[256,1440]{1,0:T(8,128)(2,1)S(1)} %reshape.50.rows_ref, bf16[256,128]{1,0:T(8,128)(2,1)S(1)} %copy-done.1, bf16[1440,1440]{1,0:T(8,128)(2,1)} %tile_hbm.1), custom_call_target="tpu_custom_call" | custom-call | tf_op jit(solution)/shard_map/pallas_call | solution.py:133
  59.0 0.0 copy-start.2
  59.0 0.0 copy-start.4
  59.0 0.2 reshape.51
  59.2 19.2 %all_to_all.21 = bf16[64,4,1440]{2,1,0:T(4,128)(2,1)S(1)} all-to-all(bf16[64,4,1440]{2,1,0:T(4,128)(2,1)S(1)} %reshape.51), channel_id=1, replica_groups=mesh['x'=4,'zh'=8,'zl'=2,'core'=2,'rep'=4] {'x','zl','core','rep'}, dimensions={0} | all-to-all | bytes 1474560 | tf_op jit(solution)/shard_map/all_to_all | solution.py:197
  78.4 0.4 reshape.52.rows_ref
  78.8 0.5 shard_map.98
  79.3 8.5 %collective-permute-start.2 = (bf16[32,1440]{1,0:T(8,128)(2,1)S(1)}, bf16[32,1440]{1,0:T(8,128)(2,1)S(1)}, u32[]{:S(2)}, u32[]{:S(2)}) collective-permute-start(bf16[32,1440]{1,0:T(8,128)(2,1)S(1)} %shard_map.98), channel_id=1, source_target_pairs={{0,0},{1,16},{2,32},{3,48},{4,64},{5,80},{6,96},{7,112},{16,1},{17... | collective-permute-start | bytes 276488 | tf_op jit(solution)/shard_map/ppermute | solution.py:206
  87.8 7.4 %collective-permute-done.2 = bf16[32,1440]{1,0:T(8,128)(2,1)S(1)} collective-permute-done((bf16[32,1440]{1,0:T(8,128)(2,1)S(1)}, bf16[32,1440]{1,0:T(8,128)(2,1)S(1)}, u32[]{:S(2)}, u32[]{:S(2)}) %collective-permute-start.2) | collective-permute-done | bytes 92192 | tf_op jit(solution)/shard_map/ppermute | solution.py:206
  95.3 12.8 %all_to_all.22 = bf16[8,16,1440]{2,1,0:T(8,128)(2,1)S(1)} all-to-all(bf16[8,16,1440]{2,1,0:T(8,128)(2,1)S(1)} %bitcast.13), channel_id=1, replica_groups=mesh['x'=4,'zh'=8,'zl'=2,'core'=2,'rep'=4] {'core','rep'}, dimensions={0} | all-to-all | bytes 737280 | tf_op jit(solution)/shard_map/all_to_all | solution.py:208
  108.1 0.1 convert_reduce_fusion
  108.1 0.0 copy-done.2
  108.1 0.0 copy-done.4
  108.1 0.0 copy-start.3
  108.2 0.7 divide_add_fusion
  108.8 0.0 copy-done.3
  (2 shorter events, 0.0 us)
Async XLA Ops:
  1.5 11.3 %collective-permute-start = (bf16[16,1440]{1,0:T(8,128)(2,1)S(1)}, bf16[16,1440]{1,0:T(8,128)(2,1)S(1)}, u32[]{:S(2)}, u32[]{:S(2)}) collective-permute-start(bf16[16,1440]{1,0:T(8,128)(2,1)S(1)} %convert_element_type.14), channel_id=1, source_target_pairs={{0,4},{4,0},{1,5},{5,1},{2,6},{6,2},{3,7},{7,3},{8,12},{12,8},{9,1... | collective-permute-start | bytes 138248 | tf_op jit(solution)/shard_map/ppermute | solution.py:165
  12.8 43.1 %copy-start = (bf16[128,256]{1,0:T(8,128)(2,1)S(1)}, bf16[128,256]{1,0:T(8,128)(2,1)}, u32[]{:S(2)}) copy-start(bf16[128,256]{1,0:T(8,128)(2,1)} %get-tuple-element.9.gather_ref) | copy-start | bytes 196612
  12.8 43.1 %copy-start.1 = (bf16[256,128]{1,0:T(8,128)(2,1)S(1)}, bf16[256,128]{1,0:T(8,128)(2,1)}, u32[]{:S(2)}) copy-start(bf16[256,128]{1,0:T(8,128)(2,1)} %get-tuple-element.11.scatter_ref) | copy-start | bytes 196612
  12.8 23.2 %collective-permute-start.1 = (bf16[32,1440]{1,0:T(8,128)(2,1)S(1)}, bf16[32,1440]{1,0:T(8,128)(2,1)S(1)}, u32[]{:S(2)}, u32[]{:S(2)}) collective-permute-start(bf16[32,1440]{1,0:T(8,128)(2,1)S(1)} %pad_maximum_fusion), channel_id=1, source_target_pairs={{0,0},{16,1},{32,2},{48,3},{64,4},{80,5},{96,6},{112,7},{1,16},{17... | collective-permute-start | bytes 276488 | tf_op jit(solution)/shard_map/ppermute | solution.py:179
  22.8 13.2 %all-to-all-start = ((s32[64,1,8]{2,1,0:T(1,128)}), s32[64,1,8]{2,1,0:T(1,128)S(1)}, u32[]{:S(2)}, u32[]{:S(2)}) async-start(s32[64,1,8]{2,1,0:T(1,128)} %bitcast.15), calls=%async_computation | async-start | bytes 65536 | tf_op jit(solution)/shard_map/all_to_all | solution.py:180
  59.0 49.1 %copy-start.2 = (f32[16,1440]{1,0:T(8,128)S(1)}, f32[16,1440]{1,0:T(8,128)}, u32[]{:S(2)}) copy-start(f32[16,1440]{1,0:T(8,128)} %param.8) | copy-start | bytes 276484
  59.0 49.1 %copy-start.4 = (f32[16,1440]{1,0:T(8,128)S(1)}, f32[16,1440]{1,0:T(8,128)}, u32[]{:S(2)}) copy-start(f32[16,1440]{1,0:T(8,128)} %param.9) | copy-start | bytes 276484
  79.3 15.9 %collective-permute-start.2 = (bf16[32,1440]{1,0:T(8,128)(2,1)S(1)}, bf16[32,1440]{1,0:T(8,128)(2,1)S(1)}, u32[]{:S(2)}, u32[]{:S(2)}) collective-permute-start(bf16[32,1440]{1,0:T(8,128)(2,1)S(1)} %shard_map.98), channel_id=1, source_target_pairs={{0,0},{1,16},{2,32},{3,48},{4,64},{5,80},{6,96},{7,112},{16,1},{17... | collective-permute-start | bytes 276488 | tf_op jit(solution)/shard_map/ppermute | solution.py:206
  108.1 0.7 copy-start.3

commit v3 on v2

v3 whole, which is shorter than its diff:
```python
import jax
import jax.numpy as jnp
from jax import lax
from jax.experimental import pallas as pl
from jax.experimental.pallas import tpu as pltpu
from jax.sharding import Mesh, PartitionSpec as P

BF = jnp.bfloat16
F32 = jnp.float32
I32 = jnp.int32
TASKS = 128
PEERS = 64
CELLS = 256
WIDTH = 1440
CHUNKS = ((0, 384), (384, 384), (768, 384), (1152, 288))
BLOCK = ("core", "x", "zl", "rep")
RING = ("zh", "core", "rep")


def iota(shape, dim):
    return lax.broadcasted_iota(I32, shape, dim)


def dot(a, b, side=1):
    return lax.dot_general(a, b, (((side,), (0,)), ((), ())), preferred_element_type=F32)


def cells(owner, rank):
    core = owner & 1
    zl = (owner >> 1) & 1
    zh = (owner >> 2) & 7
    x = owner >> 5
    peer = (((zh >> 2) * 4 + x) * 2 + zl) * 4 + (zh & 3)
    return peer * 4 + core * 2 + rank


def index_kernel(
    count_ref, ao_hbm, as_hbm, ro_hbm, rs_hbm, want_ref, place_ref,
    ao_ref, as_ref, ro_ref, rs_ref, sems,
):
    moves = [
        pltpu.make_async_copy(src, dst, sems.at[i])
        for i, (src, dst) in enumerate(
            ((ao_hbm, ao_ref), (as_hbm, as_ref), (ro_hbm, ro_ref), (rs_hbm, rs_ref))
        )
    ]
    for move in moves:
        move.start()
    for move in moves:
        move.wait()
    square = (TASKS, TASKS)
    row, col = iota(square, 0), iota(square, 1)

    def to_col(vec):
        return jnp.sum(jnp.where(row == col, vec, 0), axis=1, keepdims=True)

    live_col = iota((TASKS, 1), 0) < count_ref[0]
    live_row = iota((1, TASKS), 1) < count_ref[0]
    total = jnp.zeros((PEERS, 8), F32)
    places = []
    for which, (o_ref, s_ref) in enumerate(((ao_ref, as_ref), (ro_ref, rs_ref))):
        owner_row = o_ref[...]
        owner_col = to_col(owner_row)
        same = owner_col == owner_row
        rank_col = jnp.sum(jnp.where(same & (col < row), 1, 0), axis=1, keepdims=True)
        rank_row = jnp.sum(jnp.where(same & (row < col), 1, 0), axis=0, keepdims=True)
        place_col = cells(owner_col, rank_col)
        place_row = cells(owner_row, rank_row)
        lane = iota((TASKS, 8), 1)
        mine = (lane == (place_col & 3) + 4 * which) & live_col
        value = jnp.where(mine, to_col(s_ref[...]) + 1, 0)
        peer = jnp.where(iota((PEERS, TASKS), 0) == (place_row >> 2), 1.0, 0.0)
        total = total + dot(peer.astype(BF), value.astype(F32).astype(BF))
        places.append(jnp.where(live_row, place_row, -1))
    want_ref[...] = total.astype(I32) - 1
    which = iota((8, TASKS), 0)
    place_ref[...] = jnp.where(which == 0, places[0], places[1])


def picks(want, swap, first):
    spread = jnp.where(iota((CELLS, PEERS), 0) >> 2 == iota((CELLS, PEERS), 1), 1.0, 0.0)
    every = dot(spread.astype(BF), want.astype(F32).astype(BF)).astype(I32)
    cell = iota((CELLS, 8), 0)
    mine = iota((CELLS, 8), 1) == (cell & 3) + first
    slot = jnp.sum(jnp.where(mine, every, 0), axis=1, keepdims=True)
    part = (iota((CELLS, 1), 0) >> 1) & 1
    held = jnp.where(slot < 0, -1, jnp.bitwise_xor(part, swap) * 16 + slot)
    return jnp.where(iota((CELLS, 32), 1) == held, 1.0, 0.0).astype(BF)


def answer_kernel(half_ref, want_ref, rows_ref, out_ref):
    out_ref[...] = dot(picks(want_ref[...], half_ref[0], 0), rows_ref[...]).astype(BF).reshape(PEERS, 4, WIDTH)


def task_kernel(place_ref, rows_ref, tile_hbm, out_ref, tile_ref, sems):
    loads = [
        pltpu.make_async_copy(tile_hbm.at[pl.ds(k, n)], tile_ref.at[pl.ds(k, n)], sems.at[i])
        for i, (k, n) in enumerate(CHUNKS)
    ]
    for load in loads:
        load.start()
    cell = iota((CELLS, TASKS), 0)
    gather = jnp.where(cell == place_ref[0:1, :], 1.0, 0.0).astype(BF)
    scatter = jnp.where(cell == place_ref[1:2, :], 1.0, 0.0).astype(BF)
    operand = dot(gather, rows_ref[...], 0).astype(BF)
    total = jnp.zeros((TASKS, WIDTH), F32)
    for load, (k, n) in zip(loads, CHUNKS):
        load.wait()
        total = total + dot(operand[:, k : k + n], tile_ref[k : k + n, :])
    out_ref[...] = dot(scatter, total.astype(BF)).astype(BF).reshape(PEERS, 4, WIDTH)


def collect_kernel(want_ref, rows_ref, out_ref):
    out_ref[...] = dot(picks(want_ref[...], 0, 4), rows_ref[...].reshape(CELLS, WIDTH), 0).astype(BF)


VM = pl.BlockSpec(memory_space=pltpu.VMEM)
SM = pl.BlockSpec(memory_space=pltpu.SMEM)
HB = pl.BlockSpec(memory_space=pl.ANY)


def call(kernel, ins, outs, *args, scratch=(), limit=None):
    shapes = tuple(jax.ShapeDtypeStruct(s, d) for s, d in outs)
    return pl.pallas_call(
        kernel,
        out_shape=shapes,
        in_specs=list(ins),
        out_specs=tuple(VM for _ in shapes),
        scratch_shapes=list(scratch),
        compiler_params=pltpu.CompilerParams(vmem_limit_bytes=limit),
    )(*args)


def return_pairs():
    pairs = []
    for a in range(2):
        for b in range(4):
            for k in range(2):
                for y in range(4):
                    pairs.append((((4 * a + b) * 2 + k) * 4 + y, ((4 * k + y) * 2 + a) * 4 + b))
    return pairs


def per_device(
    amplitudes, denominators, integrals, amp_owner, amp_slot, res_owner, res_slot, task_count
):
    half = (lax.axis_index("zh") // 4).astype(I32).reshape(1)
    other = lax.optimization_barrier(lax.ppermute(amplitudes, "core", ((0, 1), (1, 0))))
    pair = jnp.concatenate([amplitudes, other]).astype(BF)
    want, place = call(
        index_kernel,
        (SM, HB, HB, HB, HB),
        (((PEERS, 8), I32), ((8, TASKS), I32)),
        task_count,
        amp_owner.reshape(1, TASKS),
        amp_slot.reshape(1, TASKS),
        res_owner.reshape(1, TASKS),
        res_slot.reshape(1, TASKS),
        scratch=[pltpu.VMEM((1, TASKS), I32)] * 4 + [pltpu.SemaphoreType.DMA((4,))],
    )
    pair, want = lax.optimization_barrier((pair, want))
    held = lax.ppermute(pair, RING, [(d, s) for s, d in return_pairs()])
    wanted = lax.all_to_all(want.reshape(PEERS, 1, 8), BLOCK, 0, 0, tiled=True).reshape(PEERS, 8)
    (found,) = call(
        answer_kernel,
        (SM, VM, VM),
        (((PEERS, 4, WIDTH), BF),),
        half,
        wanted,
        held,
        limit=16 << 20,
    )
    fetched = lax.all_to_all(found, BLOCK, 0, 0, tiled=True)
    (sent,) = call(
        task_kernel,
        (VM, VM, HB),
        (((PEERS, 4, WIDTH), BF),),
        place,
        fetched.reshape(CELLS, WIDTH),
        integrals,
        scratch=[pltpu.VMEM((WIDTH, WIDTH), BF), pltpu.SemaphoreType.DMA((len(CHUNKS),))],
        limit=50 << 20,
    )
    landed = lax.all_to_all(sent, BLOCK, 0, 0, tiled=True)
    (part,) = call(
        collect_kernel,
        (VM, VM),
        (((32, WIDTH), BF),),
        wanted,
        landed,
        limit=16 << 20,
    )
    back = lax.ppermute(part, RING, return_pairs())
    copies = jnp.broadcast_to(back.reshape(2, 1, 16, WIDTH), (2, 4, 16, WIDTH))
    every = lax.all_to_all(copies.reshape(8, 16, WIDTH), ("core", "rep"), 0, 0, tiled=True)
    residual = jnp.sum(every.astype(F32), axis=0)
    return residual, amplitudes + residual / denominators


def solution(mesh):
    fine = Mesh(mesh.devices.reshape(4, 8, 2, 2, 4), ("x", "zh", "zl", "core", "rep"))
    grid = ("x", "zh", "zl", "core")
    every = grid + ("rep",)
    return jax.shard_map(
        per_device,
        mesh=fine,
        in_specs=(
            P(grid, None),
            P(grid, None),
            P(every, None),
            P(every, None),
            P(every),
            P(every, None),
            P(every),
            P(every),
        ),
        out_specs=(P(grid, None), P(grid, None)),
        check_vma=False,
    )
```

time: 109 us -> 108 us (level)
  no operation moved by 1% of the time
where the time goes in v3:
time: 108 us; the launch traced here: 107 us
  blocking collectives  50.1 us (46%)
  starting transfers between devices  32.7 us (30%)
  waiting for transfers between devices  14.5 us (13%)
  Pallas kernels  5.95 us (6%)
  other arithmetic  1.63 us (2%)
  between operations  1.41 us (1%)
  local copies, waits for them, and re-layouts  1.09 us (1%)
    all_to_all x1, blocking collectives, per_device(): landed = lax.all_to_all(sent, BLOCK, 0, 0, tiled=True)  19.5 us
    all_to_all x1, blocking collectives, per_device(): fetched = lax.all_to_all(found, BLOCK, 0, 0, tiled=True)  18.6 us
    all_to_all x1, blocking collectives, per_device(): lax.all_to_all(copies.reshape(8, 16, WIDTH), ('core', 'rep'), 0, 0, tiled...  12.1 us
    ppermute x1, starting transfers between devices, per_device(): held = lax.ppermute(pair, RING, [(d, s) for s, d in return_pairs()])  9.97 us
    ppermute x1, starting transfers between devices, per_device(): lax.ppermute(amplitudes, 'core', ((0, 1), (1, 0)))  8.77 us
    ppermute x1, starting transfers between devices, per_device(): back = lax.ppermute(part, RING, return_pairs())  8.43 us
    all_to_all x1, waiting for transfers between devices, per_device(): lax.all_to_all(want.reshape(PEERS, 1, 8), BLOCK, 0, 0, tiled=True)  7.39 us
    ppermute x1, waiting for transfers between devices, per_device(): back = lax.ppermute(part, RING, return_pairs())  7.15 us
  transfers between devices with their start and end apart: 4, of which 2 were waited for; matrix products, arithmetic and copies ran while one was open for 0% of the time, Pallas kernels for 2%

profile of v3, /device:TPU:1, one launch (start us, length us, event | category | flops | bytes accessed | tf_op | source)
XLA Modules:
  0.0 107.5 jit_solution(1223918637881945281)
XLA Ops:
  0.6 0.9 convert.11
  1.5 8.8 %collective-permute-start = (bf16[16,1440]{1,0:T(8,128)(2,1)S(1)}, bf16[16,1440]{1,0:T(8,128)(2,1)S(1)}, u32[]{:S(2)}, u32[]{:S(2)}) collective-permute-start(bf16[16,1440]{1,0:T(8,128)(2,1)S(1)} %convert.11), channel_id=1, source_target_pairs={{0,4},{4,0},{1,5},{5,1},{2,6},{6,2},{3,7},{7,3},{8,12},{12,8},{9,1... | collective-permute-start | bytes 138248 | tf_op jit(solution)/shard_map/ppermute | solution.py:148
  11.0 1.8 %shard_map.95 = (s32[64,8]{1,0:T(8,128)}, s32[8,128]{1,0:T(8,128)}) custom-call(s32[1]{0:T(128)S(6)} %copy.12.count_ref, s32[1,128]{1,0:T(1,128)} %bitcast.16, s32[1,128]{1,0:T(1,128)} %bitcast.17, s32[1,128]{1,0:T(1,128)} %bitcast.18, s32[1,128]{1,0:T(1,128)} %bitcast.19), custom_call_target="tpu_custom_call" | custom-call | tf_op jit(solution)/shard_map/pallas_call | solution.py:124
  12.8 0.0 collective-permute-done
  12.8 10.0 %collective-permute-start.1 = (bf16[32,1440]{1,0:T(8,128)(2,1)S(1)}, bf16[32,1440]{1,0:T(8,128)(2,1)S(1)}, u32[]{:S(2)}, u32[]{:S(2)}) collective-permute-start(bf16[32,1440]{1,0:T(8,128)(2,1)S(1)} %pad_maximum_fusion), channel_id=1, source_target_pairs={{0,0},{16,1},{32,2},{48,3},{64,4},{80,5},{96,6},{112,7},{1,16},{17... | collective-permute-start | bytes 276488 | tf_op jit(solution)/shard_map/ppermute | solution.py:162
  22.8 5.5 %all-to-all-start = ((s32[64,1,8]{2,1,0:T(1,128)}), s32[64,1,8]{2,1,0:T(1,128)S(1)}, u32[]{:S(2)}, u32[]{:S(2)}) async-start(s32[64,1,8]{2,1,0:T(1,128)} %bitcast.15), calls=%async_computation | async-start | bytes 65536 | tf_op jit(solution)/shard_map/all_to_all | solution.py:163
  28.3 7.4 %all-to-all-done = s32[64,1,8]{2,1,0:T(1,128)S(1)} async-done(((s32[64,1,8]{2,1,0:T(1,128)}), s32[64,1,8]{2,1,0:T(1,128)S(1)}, u32[]{:S(2)}, u32[]{:S(2)}) %all-to-all-start) | async-done | bytes 2080 | tf_op jit(solution)/shard_map/all_to_all | solution.py:163
  35.7 0.0 collective-permute-done.1.rows_ref
  35.7 0.6 shard_map.96
  36.3 18.6 %all_to_all.20 = bf16[64,4,1440]{2,1,0:T(4,128)(2,1)S(1)} all-to-all(bf16[64,4,1440]{2,1,0:T(4,128)(2,1)S(1)} %shard_map.96), channel_id=1, replica_groups=mesh['x'=4,'zh'=8,'zl'=2,'core'=2,'rep'=4] {'core','x','zl','rep'}, dimensions={0} | all-to-all | bytes 1474560 | tf_op jit(solution)/shard_map/all_to_all | solution.py:173
  54.8 0.4 reshape.40.rows_ref
  55.2 0.0 copy-start
  55.2 0.7 copy-done
  55.9 0.0 copy-start.1
  55.9 0.0 copy-start.3
  55.9 3.1 %shard_map.97 = bf16[64,4,1440]{2,1,0:T(4,128)(2,1)S(1)} custom-call(s32[8,128]{1,0:T(8,128)S(1)} %copy-done, bf16[256,1440]{1,0:T(8,128)(2,1)S(1)} %reshape.40.rows_ref, bf16[1440,1440]{1,0:T(8,128)(2,1)} %tile_hbm.1), custom_call_target="tpu_custom_call" | custom-call | tf_op jit(solution)/shard_map/pallas_call | solution.py:124
  59.0 19.5 %all_to_all.21.rows_ref = bf16[64,4,1440]{2,1,0:T(4,128)(2,1)S(1)} all-to-all(bf16[64,4,1440]{2,1,0:T(4,128)(2,1)S(1)} %shard_map.97), channel_id=1, replica_groups=mesh['x'=4,'zh'=8,'zl'=2,'core'=2,'rep'=4] {'core','x','zl','rep'}, dimensions={0} | all-to-all | bytes 1474560 | tf_op jit(solution)/shard_map/all_to_all | solution.py:184
  78.5 0.5 shard_map.98
  79.0 8.4 %collective-permute-start.2 = (bf16[32,1440]{1,0:T(8,128)(2,1)S(1)}, bf16[32,1440]{1,0:T(8,128)(2,1)S(1)}, u32[]{:S(2)}, u32[]{:S(2)}) collective-permute-start(bf16[32,1440]{1,0:T(8,128)(2,1)S(1)} %shard_map.98), channel_id=1, source_target_pairs={{0,0},{1,16},{2,32},{3,48},{4,64},{5,80},{6,96},{7,112},{16,1},{17... | collective-permute-start | bytes 276488 | tf_op jit(solution)/shard_map/ppermute | solution.py:193
  87.5 7.1 %collective-permute-done.2 = bf16[32,1440]{1,0:T(8,128)(2,1)S(1)} collective-permute-done((bf16[32,1440]{1,0:T(8,128)(2,1)S(1)}, bf16[32,1440]{1,0:T(8,128)(2,1)S(1)}, u32[]{:S(2)}, u32[]{:S(2)}) %collective-permute-start.2) | collective-permute-done | bytes 92192 | tf_op jit(solution)/shard_map/ppermute | solution.py:193
  94.6 12.1 %all_to_all.22 = bf16[8,16,1440]{2,1,0:T(8,128)(2,1)S(1)} all-to-all(bf16[8,16,1440]{2,1,0:T(8,128)(2,1)S(1)} %bitcast.13), channel_id=1, replica_groups=mesh['x'=4,'zh'=8,'zl'=2,'core'=2,'rep'=4] {'core','rep'}, dimensions={0} | all-to-all | bytes 737280 | tf_op jit(solution)/shard_map/all_to_all | solution.py:195
  106.7 0.1 convert_reduce_fusion
  106.8 0.0 copy-done.1
  106.8 0.0 copy-done.3
  106.8 0.0 copy-start.2
  106.8 0.7 divide_add_fusion
  107.5 0.0 copy-done.2
  (2 shorter events, 0.0 us)
Async XLA Ops:
  1.5 11.2 %collective-permute-start = (bf16[16,1440]{1,0:T(8,128)(2,1)S(1)}, bf16[16,1440]{1,0:T(8,128)(2,1)S(1)}, u32[]{:S(2)}, u32[]{:S(2)}) collective-permute-start(bf16[16,1440]{1,0:T(8,128)(2,1)S(1)} %convert.11), channel_id=1, source_target_pairs={{0,4},{4,0},{1,5},{5,1},{2,6},{6,2},{3,7},{7,3},{8,12},{12,8},{9,1... | collective-permute-start | bytes 138248 | tf_op jit(solution)/shard_map/ppermute | solution.py:148
  12.8 22.9 %collective-permute-start.1 = (bf16[32,1440]{1,0:T(8,128)(2,1)S(1)}, bf16[32,1440]{1,0:T(8,128)(2,1)S(1)}, u32[]{:S(2)}, u32[]{:S(2)}) collective-permute-start(bf16[32,1440]{1,0:T(8,128)(2,1)S(1)} %pad_maximum_fusion), channel_id=1, source_target_pairs={{0,0},{16,1},{32,2},{48,3},{64,4},{80,5},{96,6},{112,7},{1,16},{17... | collective-permute-start | bytes 276488 | tf_op jit(solution)/shard_map/ppermute | solution.py:162
  22.8 13.0 %all-to-all-start = ((s32[64,1,8]{2,1,0:T(1,128)}), s32[64,1,8]{2,1,0:T(1,128)S(1)}, u32[]{:S(2)}, u32[]{:S(2)}) async-start(s32[64,1,8]{2,1,0:T(1,128)} %bitcast.15), calls=%async_computation | async-start | bytes 65536 | tf_op jit(solution)/shard_map/all_to_all | solution.py:163
  55.2 0.7 copy-start
  55.9 50.9 %copy-start.1 = (f32[16,1440]{1,0:T(8,128)S(1)}, f32[16,1440]{1,0:T(8,128)}, u32[]{:S(2)}) copy-start(f32[16,1440]{1,0:T(8,128)} %param.8) | copy-start | bytes 276484
  55.9 50.9 %copy-start.3 = (f32[16,1440]{1,0:T(8,128)S(1)}, f32[16,1440]{1,0:T(8,128)}, u32[]{:S(2)}) copy-start(f32[16,1440]{1,0:T(8,128)} %param.9) | copy-start | bytes 276484
  79.0 15.6 %collective-permute-start.2 = (bf16[32,1440]{1,0:T(8,128)(2,1)S(1)}, bf16[32,1440]{1,0:T(8,128)(2,1)S(1)}, u32[]{:S(2)}, u32[]{:S(2)}) collective-permute-start(bf16[32,1440]{1,0:T(8,128)(2,1)S(1)} %shard_map.98), channel_id=1, source_target_pairs={{0,0},{1,16},{2,32},{3,48},{4,64},{5,80},{6,96},{7,112},{16,1},{17... | collective-permute-start | bytes 276488 | tf_op jit(solution)/shard_map/ppermute | solution.py:193
  106.8 0.7 copy-start.2

commit v4 on v3

--- a/solution.py
+++ b/solution.py
@@ -54,24 +54,24 @@
     def to_col(vec):
         return jnp.sum(jnp.where(row == col, vec, 0), axis=1, keepdims=True)
 
-    live_col = iota((TASKS, 1), 0) < count_ref[0]
     live_row = iota((1, TASKS), 1) < count_ref[0]
     total = jnp.zeros((PEERS, 8), F32)
     places = []
     for which, (o_ref, s_ref) in enumerate(((ao_ref, as_ref), (ro_ref, rs_ref))):
         owner_row = o_ref[...]
-        owner_col = to_col(owner_row)
-        same = owner_col == owner_row
-        rank_col = jnp.sum(jnp.where(same & (col < row), 1, 0), axis=1, keepdims=True)
-        rank_row = jnp.sum(jnp.where(same & (row < col), 1, 0), axis=0, keepdims=True)
-        place_col = cells(owner_col, rank_col)
-        place_row = cells(owner_row, rank_row)
-        lane = iota((TASKS, 8), 1)
-        mine = (lane == (place_col & 3) + 4 * which) & live_col
-        value = jnp.where(mine, to_col(s_ref[...]) + 1, 0)
-        peer = jnp.where(iota((PEERS, TASKS), 0) == (place_row >> 2), 1.0, 0.0)
-        total = total + dot(peer.astype(BF), value.astype(F32).astype(BF))
-        places.append(jnp.where(live_row, place_row, -1))
+        same = to_col(owner_row) == owner_row
+        rank = jnp.sum(jnp.where(same & (row < col), 1, 0), axis=0, keepdims=True)
+        place = cells(owner_row, rank)
+        mine = (iota((8, TASKS), 0) == (place & 3) + 4 * which) & live_row
+        value = jnp.where(mine, s_ref[...] + 1, 0)
+        peer = jnp.where(iota((PEERS, TASKS), 0) == (place >> 2), 1.0, 0.0)
+        total = total + lax.dot_general(
+            peer.astype(BF),
+            value.astype(F32).astype(BF),
+            (((1,), (1,)), ((), ())),
+            preferred_element_type=F32,
+        )
+        places.append(jnp.where(live_row, place, -1))
     want_ref[...] = total.astype(I32) - 1
     which = iota((8, TASKS), 0)
     place_ref[...] = jnp.where(which == 0, places[0], places[1])
@@ -88,7 +88,8 @@
     return jnp.where(iota((CELLS, 32), 1) == held, 1.0, 0.0).astype(BF)
 
 
-def answer_kernel(half_ref, want_ref, rows_ref, out_ref):
+def answer_kernel(half_ref, want_ref, rows_ref, place_ref, out_ref, place_out_ref):
+    place_out_ref[...] = place_ref[...]
     out_ref[...] = dot(picks(want_ref[...], half_ref[0], 0), rows_ref[...]).astype(BF).reshape(PEERS, 4, WIDTH)
 
 
@@ -102,7 +103,7 @@
     cell = iota((CELLS, TASKS), 0)
     gather = jnp.where(cell == place_ref[0:1, :], 1.0, 0.0).astype(BF)
     scatter = jnp.where(cell == place_ref[1:2, :], 1.0, 0.0).astype(BF)
-    operand = dot(gather, rows_ref[...], 0).astype(BF)
+    operand = dot(gather, rows_ref[...].reshape(CELLS, WIDTH), 0).astype(BF)
     total = jnp.zeros((TASKS, WIDTH), F32)
     for load, (k, n) in zip(loads, CHUNKS):
         load.wait()
@@ -161,13 +162,14 @@
     pair, want = lax.optimization_barrier((pair, want))
     held = lax.ppermute(pair, RING, [(d, s) for s, d in return_pairs()])
     wanted = lax.all_to_all(want.reshape(PEERS, 1, 8), BLOCK, 0, 0, tiled=True).reshape(PEERS, 8)
-    (found,) = call(
+    found, place = call(
         answer_kernel,
-        (SM, VM, VM),
-        (((PEERS, 4, WIDTH), BF),),
+        (SM, VM, VM, VM),
+        (((PEERS, 4, WIDTH), BF), ((8, TASKS), I32)),
         half,
         wanted,
         held,
+        place,
         limit=16 << 20,
     )
     fetched = lax.all_to_all(found, BLOCK, 0, 0, tiled=True)
@@ -176,7 +178,7 @@
         (VM, VM, HB),
         (((PEERS, 4, WIDTH), BF),),
         place,
-        fetched.reshape(CELLS, WIDTH),
+        fetched,
         integrals,
         scratch=[pltpu.VMEM((WIDTH, WIDTH), BF), pltpu.SemaphoreType.DMA((len(CHUNKS),))],
         limit=50 << 20,

time: 108 us -> 107 us (level)
  no operation moved by 1% of the time
where the time goes in v4:
time: 107 us
  blocking collectives  50.1 us (47%)
  starting transfers between devices  32.7 us (31%)
  waiting for transfers between devices  14.6 us (14%)
  Pallas kernels  5.81 us (5%)
  other arithmetic  1.63 us (2%)
  between operations  1.4 us (1%)
    all_to_all x1, blocking collectives, per_device(): landed = lax.all_to_all(sent, BLOCK, 0, 0, tiled=True)  19.5 us
    all_to_all x1, blocking collectives, per_device(): fetched = lax.all_to_all(found, BLOCK, 0, 0, tiled=True)  18.6 us
    all_to_all x1, blocking collectives, per_device(): lax.all_to_all(copies.reshape(8, 16, WIDTH), ('core', 'rep'), 0, 0, tiled...  12.1 us
    ppermute x1, starting transfers between devices, per_device(): held = lax.ppermute(pair, RING, [(d, s) for s, d in return_pairs()])  9.97 us
    ppermute x1, starting transfers between devices, per_device(): lax.ppermute(amplitudes, 'core', ((0, 1), (1, 0)))  8.77 us
    ppermute x1, starting transfers between devices, per_device(): back = lax.ppermute(part, RING, return_pairs())  8.42 us
    all_to_all x1, waiting for transfers between devices, per_device(): lax.all_to_all(want.reshape(PEERS, 1, 8), BLOCK, 0, 0, tiled=True)  7.39 us
    ppermute x1, waiting for transfers between devices, per_device(): back = lax.ppermute(part, RING, return_pairs())  7.16 us
  transfers between devices with their start and end apart: 4, of which 2 were waited for; matrix products, arithmetic and copies ran while one was open for 0% of the time, Pallas kernels for 2%

profile of v4, /device:TPU:1, one launch (start us, length us, event | category | flops | bytes accessed | tf_op | source)
XLA Modules:
  0.0 107.0 jit_solution(3061032709349801169)
XLA Ops:
  0.6 0.9 convert.11
  1.5 8.8 %collective-permute-start = (bf16[16,1440]{1,0:T(8,128)(2,1)S(1)}, bf16[16,1440]{1,0:T(8,128)(2,1)S(1)}, u32[]{:S(2)}, u32[]{:S(2)}) collective-permute-start(bf16[16,1440]{1,0:T(8,128)(2,1)S(1)} %convert.11), channel_id=1, source_target_pairs={{0,4},{4,0},{1,5},{5,1},{2,6},{6,2},{3,7},{7,3},{8,12},{12,8},{9,1... | collective-permute-start | bytes 138248 | tf_op jit(solution)/shard_map/ppermute | solution.py:149
  11.0 1.6 %shard_map.95 = (s32[64,8]{1,0:T(8,128)}, s32[8,128]{1,0:T(8,128)}) custom-call(s32[1]{0:T(128)S(6)} %copy.12.count_ref, s32[1,128]{1,0:T(1,128)} %bitcast.16, s32[1,128]{1,0:T(1,128)} %bitcast.17, s32[1,128]{1,0:T(1,128)} %bitcast.18, s32[1,128]{1,0:T(1,128)} %bitcast.19), custom_call_target="tpu_custom_call" | custom-call | tf_op jit(solution)/shard_map/pallas_call | solution.py:125
  12.6 0.0 collective-permute-done
  12.6 10.0 %collective-permute-start.1 = (bf16[32,1440]{1,0:T(8,128)(2,1)S(1)}, bf16[32,1440]{1,0:T(8,128)(2,1)S(1)}, u32[]{:S(2)}, u32[]{:S(2)}) collective-permute-start(bf16[32,1440]{1,0:T(8,128)(2,1)S(1)} %pad_maximum_fusion), channel_id=1, source_target_pairs={{0,0},{16,1},{32,2},{48,3},{64,4},{80,5},{96,6},{112,7},{1,16},{17... | collective-permute-start | bytes 276488 | tf_op jit(solution)/shard_map/ppermute | solution.py:163
  22.6 5.5 %all-to-all-start = ((s32[64,1,8]{2,1,0:T(1,128)}), s32[64,1,8]{2,1,0:T(1,128)S(1)}, u32[]{:S(2)}, u32[]{:S(2)}) async-start(s32[64,1,8]{2,1,0:T(1,128)} %bitcast.15), calls=%async_computation | async-start | bytes 65536 | tf_op jit(solution)/shard_map/all_to_all | solution.py:164
  28.2 7.4 %all-to-all-done = s32[64,1,8]{2,1,0:T(1,128)S(1)} async-done(((s32[64,1,8]{2,1,0:T(1,128)}), s32[64,1,8]{2,1,0:T(1,128)S(1)}, u32[]{:S(2)}, u32[]{:S(2)}) %all-to-all-start) | async-done | bytes 2080 | tf_op jit(solution)/shard_map/all_to_all | solution.py:164
  35.6 0.0 collective-permute-done.1.rows_ref
  35.6 0.0 copy-start
  35.6 0.7 copy-done
  36.3 0.5 shard_map.96
  36.8 18.6 %all_to_all.20.rows_ref = bf16[64,4,1440]{2,1,0:T(4,128)(2,1)S(1)} all-to-all(bf16[64,4,1440]{2,1,0:T(4,128)(2,1)S(1)} %get-tuple-element.13), channel_id=1, replica_groups=mesh['x'=4,'zh'=8,'zl'=2,'core'=2,'rep'=4] {'core','x','zl','rep'}, dimensions={0} | all-to-all | bytes 1474560 | tf_op jit(solution)/shard_map/all_to_all | solution.py:175
  55.4 0.0 copy-start.1
  55.4 0.0 copy-start.3
  55.4 3.1 %shard_map.97 = bf16[64,4,1440]{2,1,0:T(4,128)(2,1)S(1)} custom-call(s32[8,128]{1,0:T(8,128)S(1)} %get-tuple-element.12.place_ref, bf16[64,4,1440]{2,1,0:T(4,128)(2,1)S(1)} %all_to_all.20.rows_ref, bf16[1440,1440]{1,0:T(8,128)(2,1)} %tile_hbm.1), custom_call_target="tpu_custom_call" | custom-call | tf_op jit(solution)/shard_map/pallas_call | solution.py:125
  58.5 19.5 %all_to_all.21.rows_ref = bf16[64,4,1440]{2,1,0:T(4,128)(2,1)S(1)} all-to-all(bf16[64,4,1440]{2,1,0:T(4,128)(2,1)S(1)} %shard_map.97), channel_id=1, replica_groups=mesh['x'=4,'zh'=8,'zl'=2,'core'=2,'rep'=4] {'core','x','zl','rep'}, dimensions={0} | all-to-all | bytes 1474560 | tf_op jit(solution)/shard_map/all_to_all | solution.py:186
  78.0 0.5 shard_map.98
  78.5 8.4 %collective-permute-start.2 = (bf16[32,1440]{1,0:T(8,128)(2,1)S(1)}, bf16[32,1440]{1,0:T(8,128)(2,1)S(1)}, u32[]{:S(2)}, u32[]{:S(2)}) collective-permute-start(bf16[32,1440]{1,0:T(8,128)(2,1)S(1)} %shard_map.98), channel_id=1, source_target_pairs={{0,0},{1,16},{2,32},{3,48},{4,64},{5,80},{6,96},{7,112},{16,1},{17... | collective-permute-start | bytes 276488 | tf_op jit(solution)/shard_map/ppermute | solution.py:195
  86.9 7.2 %collective-permute-done.2 = bf16[32,1440]{1,0:T(8,128)(2,1)S(1)} collective-permute-done((bf16[32,1440]{1,0:T(8,128)(2,1)S(1)}, bf16[32,1440]{1,0:T(8,128)(2,1)S(1)}, u32[]{:S(2)}, u32[]{:S(2)}) %collective-permute-start.2) | collective-permute-done | bytes 92192 | tf_op jit(solution)/shard_map/ppermute | solution.py:195
  94.1 12.1 %all_to_all.22 = bf16[8,16,1440]{2,1,0:T(8,128)(2,1)S(1)} all-to-all(bf16[8,16,1440]{2,1,0:T(8,128)(2,1)S(1)} %bitcast.13), channel_id=1, replica_groups=mesh['x'=4,'zh'=8,'zl'=2,'core'=2,'rep'=4] {'core','rep'}, dimensions={0} | all-to-all | bytes 737280 | tf_op jit(solution)/shard_map/all_to_all | solution.py:197
  106.2 0.1 convert_reduce_fusion
  106.3 0.0 copy-done.1
  106.3 0.0 copy-done.3
  106.3 0.0 copy-start.2
  106.3 0.7 divide_add_fusion
  107.0 0.0 copy-done.2
  (2 shorter events, 0.0 us)
Async XLA Ops:
  1.5 11.1 %collective-permute-start = (bf16[16,1440]{1,0:T(8,128)(2,1)S(1)}, bf16[16,1440]{1,0:T(8,128)(2,1)S(1)}, u32[]{:S(2)}, u32[]{:S(2)}) collective-permute-start(bf16[16,1440]{1,0:T(8,128)(2,1)S(1)} %convert.11), channel_id=1, source_target_pairs={{0,4},{4,0},{1,5},{5,1},{2,6},{6,2},{3,7},{7,3},{8,12},{12,8},{9,1... | collective-permute-start | bytes 138248 | tf_op jit(solution)/shard_map/ppermute | solution.py:149
  12.6 22.9 %collective-permute-start.1 = (bf16[32,1440]{1,0:T(8,128)(2,1)S(1)}, bf16[32,1440]{1,0:T(8,128)(2,1)S(1)}, u32[]{:S(2)}, u32[]{:S(2)}) collective-permute-start(bf16[32,1440]{1,0:T(8,128)(2,1)S(1)} %pad_maximum_fusion), channel_id=1, source_target_pairs={{0,0},{16,1},{32,2},{48,3},{64,4},{80,5},{96,6},{112,7},{1,16},{17... | collective-permute-start | bytes 276488 | tf_op jit(solution)/shard_map/ppermute | solution.py:163
  22.6 13.0 %all-to-all-start = ((s32[64,1,8]{2,1,0:T(1,128)}), s32[64,1,8]{2,1,0:T(1,128)S(1)}, u32[]{:S(2)}, u32[]{:S(2)}) async-start(s32[64,1,8]{2,1,0:T(1,128)} %bitcast.15), calls=%async_computation | async-start | bytes 65536 | tf_op jit(solution)/shard_map/all_to_all | solution.py:164
  35.6 0.7 copy-start
  55.4 50.9 %copy-start.1 = (f32[16,1440]{1,0:T(8,128)S(1)}, f32[16,1440]{1,0:T(8,128)}, u32[]{:S(2)}) copy-start(f32[16,1440]{1,0:T(8,128)} %param.8) | copy-start | bytes 276484
  55.4 50.9 %copy-start.3 = (f32[16,1440]{1,0:T(8,128)S(1)}, f32[16,1440]{1,0:T(8,128)}, u32[]{:S(2)}) copy-start(f32[16,1440]{1,0:T(8,128)} %param.9) | copy-start | bytes 276484
  78.5 15.6 %collective-permute-start.2 = (bf16[32,1440]{1,0:T(8,128)(2,1)S(1)}, bf16[32,1440]{1,0:T(8,128)(2,1)S(1)}, u32[]{:S(2)}, u32[]{:S(2)}) collective-permute-start(bf16[32,1440]{1,0:T(8,128)(2,1)S(1)} %shard_map.98), channel_id=1, source_target_pairs={{0,0},{1,16},{2,32},{3,48},{4,64},{5,80},{6,96},{7,112},{16,1},{17... | collective-permute-start | bytes 276488 | tf_op jit(solution)/shard_map/ppermute | solution.py:195
  106.3 0.7 copy-start.2

commit v5 on v4

--- a/solution.py
+++ b/solution.py
@@ -132,13 +132,28 @@
     )(*args)
 
 
+LANDING = ((2, 0), (3, 1), (1, 1), (0, 1), (0, 0), (1, 0), (3, 0), (2, 1))
+
+
 def return_pairs():
+    pairs = []
+    for zh in range(8):
+        for core in range(2):
+            for rep in range(4):
+                home = 4 * core + rep
+                step, to_core = LANDING[(zh - home) % 8]
+                target = (home * 2 + to_core) * 4 + (rep + step) % 4
+                pairs.append(((zh * 2 + core) * 4 + rep, target))
+    return pairs
+
+
+def spread_pairs():
     pairs = []
     for a in range(2):
         for b in range(4):
             for k in range(2):
                 for y in range(4):
-                    pairs.append((((4 * a + b) * 2 + k) * 4 + y, ((4 * k + y) * 2 + a) * 4 + b))
+                    pairs.append((((4 * a + b) * 2 + k) * 4 + y, ((4 * k + y) * 2 + a) * 4 + (b ^ y)))
     return pairs
 
 
@@ -160,7 +175,7 @@
         scratch=[pltpu.VMEM((1, TASKS), I32)] * 4 + [pltpu.SemaphoreType.DMA((4,))],
     )
     pair, want = lax.optimization_barrier((pair, want))
-    held = lax.ppermute(pair, RING, [(d, s) for s, d in return_pairs()])
+    held = lax.ppermute(pair, RING, [(d, s) for s, d in spread_pairs()])
     wanted = lax.all_to_all(want.reshape(PEERS, 1, 8), BLOCK, 0, 0, tiled=True).reshape(PEERS, 8)
     found, place = call(
         answer_kernel,

time: 107 us -> 107 us (level)
  waiting for transfers between devices: 14.6 us -> 11 us
  blocking collectives: 50.1 us -> 53.3 us
    ppermute x1, waiting for transfers between devices: 7.16 us -> 3.63 us  [per_device(): back = lax.ppermute(part, RING, return_pairs())]
    all_to_all x1, blocking collectives: 12.1 us -> 15.2 us  [per_device(): lax.all_to_all(copies.reshape(8, 16, WIDTH), ('core', 'rep'), 0, 0, tiled...]
where the time goes in v5:
time: 107 us; the launch traced here: 106 us
  blocking collectives  53.3 us (50%)
  starting transfers between devices  32.5 us (30%)
  waiting for transfers between devices  11 us (10%)
  Pallas kernels  5.81 us (5%)
  other arithmetic  1.63 us (2%)
  between operations  1.4 us (1%)
    all_to_all x1, blocking collectives, per_device(): landed = lax.all_to_all(sent, BLOCK, 0, 0, tiled=True)  19.5 us
    all_to_all x1, blocking collectives, per_device(): fetched = lax.all_to_all(found, BLOCK, 0, 0, tiled=True)  18.6 us
    all_to_all x1, blocking collectives, per_device(): lax.all_to_all(copies.reshape(8, 16, WIDTH), ('core', 'rep'), 0, 0, tiled...  15.2 us
    ppermute x1, starting transfers between devices, per_device(): held = lax.ppermute(pair, RING, [(d, s) for s, d in spread_pairs()])  9.97 us
    ppermute x1, starting transfers between devices, per_device(): lax.ppermute(amplitudes, 'core', ((0, 1), (1, 0)))  8.77 us
    ppermute x1, starting transfers between devices, per_device(): back = lax.ppermute(part, RING, return_pairs())  8.21 us
    all_to_all x1, waiting for transfers between devices, per_device(): lax.all_to_all(want.reshape(PEERS, 1, 8), BLOCK, 0, 0, tiled=True)  7.39 us
    pallas_call x4, Pallas kernels, call(): pl.pallas_call(kernel, out_shape=shapes, in_specs=list(ins), out_specs=tu...  5.81 us
  transfers between devices with their start and end apart: 4, of which 2 were waited for; matrix products, arithmetic and copies ran while one was open for 0% of the time, Pallas kernels for 2%

profile of v5, /device:TPU:1, one launch (start us, length us, event | category | flops | bytes accessed | tf_op | source)
XLA Modules:
  0.0 106.4 jit_solution(9026931723231305343)
XLA Ops:
  0.6 0.9 convert.11
  1.5 8.8 %collective-permute-start = (bf16[16,1440]{1,0:T(8,128)(2,1)S(1)}, bf16[16,1440]{1,0:T(8,128)(2,1)S(1)}, u32[]{:S(2)}, u32[]{:S(2)}) collective-permute-start(bf16[16,1440]{1,0:T(8,128)(2,1)S(1)} %convert.11), channel_id=1, source_target_pairs={{0,4},{4,0},{1,5},{5,1},{2,6},{6,2},{3,7},{7,3},{8,12},{12,8},{9,1... | collective-permute-start | bytes 138248 | tf_op jit(solution)/shard_map/ppermute | solution.py:164
  11.0 1.6 %shard_map.95 = (s32[64,8]{1,0:T(8,128)}, s32[8,128]{1,0:T(8,128)}) custom-call(s32[1]{0:T(128)S(6)} %copy.12.count_ref, s32[1,128]{1,0:T(1,128)} %bitcast.16, s32[1,128]{1,0:T(1,128)} %bitcast.17, s32[1,128]{1,0:T(1,128)} %bitcast.18, s32[1,128]{1,0:T(1,128)} %bitcast.19), custom_call_target="tpu_custom_call" | custom-call | tf_op jit(solution)/shard_map/pallas_call | solution.py:125
  12.6 0.0 collective-permute-done
  12.6 10.0 %collective-permute-start.1 = (bf16[32,1440]{1,0:T(8,128)(2,1)S(1)}, bf16[32,1440]{1,0:T(8,128)(2,1)S(1)}, u32[]{:S(2)}, u32[]{:S(2)}) collective-permute-start(bf16[32,1440]{1,0:T(8,128)(2,1)S(1)} %pad_maximum_fusion), channel_id=1, source_target_pairs={{0,0},{17,1},{34,2},{51,3},{64,4},{81,5},{98,6},{115,7},{1,16},{16... | collective-permute-start | bytes 276488 | tf_op jit(solution)/shard_map/ppermute | solution.py:178
  22.6 5.5 %all-to-all-start = ((s32[64,1,8]{2,1,0:T(1,128)}), s32[64,1,8]{2,1,0:T(1,128)S(1)}, u32[]{:S(2)}, u32[]{:S(2)}) async-start(s32[64,1,8]{2,1,0:T(1,128)} %bitcast.15), calls=%async_computation | async-start | bytes 65536 | tf_op jit(solution)/shard_map/all_to_all | solution.py:179
  28.2 7.4 %all-to-all-done = s32[64,1,8]{2,1,0:T(1,128)S(1)} async-done(((s32[64,1,8]{2,1,0:T(1,128)}), s32[64,1,8]{2,1,0:T(1,128)S(1)}, u32[]{:S(2)}, u32[]{:S(2)}) %all-to-all-start) | async-done | bytes 2080 | tf_op jit(solution)/shard_map/all_to_all | solution.py:179
  35.6 0.0 collective-permute-done.1.rows_ref
  35.6 0.0 copy-start
  35.6 0.7 copy-done
  36.3 0.5 shard_map.96
  36.8 18.6 %all_to_all.20.rows_ref = bf16[64,4,1440]{2,1,0:T(4,128)(2,1)S(1)} all-to-all(bf16[64,4,1440]{2,1,0:T(4,128)(2,1)S(1)} %get-tuple-element.13), channel_id=1, replica_groups=mesh['x'=4,'zh'=8,'zl'=2,'core'=2,'rep'=4] {'core','x','zl','rep'}, dimensions={0} | all-to-all | bytes 1474560 | tf_op jit(solution)/shard_map/all_to_all | solution.py:190
  55.4 0.0 copy-start.1
  55.4 0.0 copy-start.3
  55.4 3.1 %shard_map.97 = bf16[64,4,1440]{2,1,0:T(4,128)(2,1)S(1)} custom-call(s32[8,128]{1,0:T(8,128)S(1)} %get-tuple-element.12.place_ref, bf16[64,4,1440]{2,1,0:T(4,128)(2,1)S(1)} %all_to_all.20.rows_ref, bf16[1440,1440]{1,0:T(8,128)(2,1)} %tile_hbm.1), custom_call_target="tpu_custom_call" | custom-call | tf_op jit(solution)/shard_map/pallas_call | solution.py:125
  58.5 19.5 %all_to_all.21.rows_ref = bf16[64,4,1440]{2,1,0:T(4,128)(2,1)S(1)} all-to-all(bf16[64,4,1440]{2,1,0:T(4,128)(2,1)S(1)} %shard_map.97), channel_id=1, replica_groups=mesh['x'=4,'zh'=8,'zl'=2,'core'=2,'rep'=4] {'core','x','zl','rep'}, dimensions={0} | all-to-all | bytes 1474560 | tf_op jit(solution)/shard_map/all_to_all | solution.py:201
  78.0 0.5 shard_map.98
  78.5 8.2 %collective-permute-start.2 = (bf16[32,1440]{1,0:T(8,128)(2,1)S(1)}, bf16[32,1440]{1,0:T(8,128)(2,1)S(1)}, u32[]{:S(2)}, u32[]{:S(2)}) collective-permute-start(bf16[32,1440]{1,0:T(8,128)(2,1)S(1)} %shard_map.98), channel_id=1, source_target_pairs={{0,2},{1,23},{2,33},{3,48},{4,64},{5,85},{6,103},{7,118},{16,7},{1... | collective-permute-start | bytes 276488 | tf_op jit(solution)/shard_map/ppermute | solution.py:210
  86.7 3.6 %collective-permute-done.2 = bf16[32,1440]{1,0:T(8,128)(2,1)S(1)} collective-permute-done((bf16[32,1440]{1,0:T(8,128)(2,1)S(1)}, bf16[32,1440]{1,0:T(8,128)(2,1)S(1)}, u32[]{:S(2)}, u32[]{:S(2)}) %collective-permute-start.2) | collective-permute-done | bytes 92192 | tf_op jit(solution)/shard_map/ppermute | solution.py:210
  90.4 15.2 %all_to_all.22 = bf16[8,16,1440]{2,1,0:T(8,128)(2,1)S(1)} all-to-all(bf16[8,16,1440]{2,1,0:T(8,128)(2,1)S(1)} %bitcast.13), channel_id=1, replica_groups=mesh['x'=4,'zh'=8,'zl'=2,'core'=2,'rep'=4] {'core','rep'}, dimensions={0} | all-to-all | bytes 737280 | tf_op jit(solution)/shard_map/all_to_all | solution.py:212
  105.6 0.1 convert_reduce_fusion
  105.7 0.0 copy-done.1
  105.7 0.0 copy-done.3
  105.7 0.0 copy-start.2
  105.7 0.7 divide_add_fusion
  106.4 0.0 copy-done.2
  (2 shorter events, 0.0 us)
Async XLA Ops:
  1.5 11.1 %collective-permute-start = (bf16[16,1440]{1,0:T(8,128)(2,1)S(1)}, bf16[16,1440]{1,0:T(8,128)(2,1)S(1)}, u32[]{:S(2)}, u32[]{:S(2)}) collective-permute-start(bf16[16,1440]{1,0:T(8,128)(2,1)S(1)} %convert.11), channel_id=1, source_target_pairs={{0,4},{4,0},{1,5},{5,1},{2,6},{6,2},{3,7},{7,3},{8,12},{12,8},{9,1... | collective-permute-start | bytes 138248 | tf_op jit(solution)/shard_map/ppermute | solution.py:164
  12.6 22.9 %collective-permute-start.1 = (bf16[32,1440]{1,0:T(8,128)(2,1)S(1)}, bf16[32,1440]{1,0:T(8,128)(2,1)S(1)}, u32[]{:S(2)}, u32[]{:S(2)}) collective-permute-start(bf16[32,1440]{1,0:T(8,128)(2,1)S(1)} %pad_maximum_fusion), channel_id=1, source_target_pairs={{0,0},{17,1},{34,2},{51,3},{64,4},{81,5},{98,6},{115,7},{1,16},{16... | collective-permute-start | bytes 276488 | tf_op jit(solution)/shard_map/ppermute | solution.py:178
  22.6 13.0 %all-to-all-start = ((s32[64,1,8]{2,1,0:T(1,128)}), s32[64,1,8]{2,1,0:T(1,128)S(1)}, u32[]{:S(2)}, u32[]{:S(2)}) async-start(s32[64,1,8]{2,1,0:T(1,128)} %bitcast.15), calls=%async_computation | async-start | bytes 65536 | tf_op jit(solution)/shard_map/all_to_all | solution.py:179
  35.6 0.7 copy-start
  55.4 50.3 %copy-start.1 = (f32[16,1440]{1,0:T(8,128)S(1)}, f32[16,1440]{1,0:T(8,128)}, u32[]{:S(2)}) copy-start(f32[16,1440]{1,0:T(8,128)} %param.8) | copy-start | bytes 276484
  55.4 50.3 %copy-start.3 = (f32[16,1440]{1,0:T(8,128)S(1)}, f32[16,1440]{1,0:T(8,128)}, u32[]{:S(2)}) copy-start(f32[16,1440]{1,0:T(8,128)} %param.9) | copy-start | bytes 276484
  78.5 11.9 %collective-permute-start.2 = (bf16[32,1440]{1,0:T(8,128)(2,1)S(1)}, bf16[32,1440]{1,0:T(8,128)(2,1)S(1)}, u32[]{:S(2)}, u32[]{:S(2)}) collective-permute-start(bf16[32,1440]{1,0:T(8,128)(2,1)S(1)} %shard_map.98), channel_id=1, source_target_pairs={{0,2},{1,23},{2,33},{3,48},{4,64},{5,85},{6,103},{7,118},{16,7},{1... | collective-permute-start | bytes 276488 | tf_op jit(solution)/shard_map/ppermute | solution.py:210
  105.7 0.7 copy-start.2

commit v6 on v5

--- a/solution.py
+++ b/solution.py
@@ -121,7 +121,9 @@
 
 
 def call(kernel, ins, outs, *args, scratch=(), limit=None):
-    shapes = tuple(jax.ShapeDtypeStruct(s, d) for s, d in outs)
+    shapes = tuple(
+        pltpu.VMEM(s, d) if s == (8, TASKS) else jax.ShapeDtypeStruct(s, d) for s, d in outs
+    )
     return pl.pallas_call(
         kernel,
         out_shape=shapes,

time: 107 us -> 106 us (level)
  no operation moved by 1% of the time
where the time goes in v6:
time: 106 us
  blocking collectives  53.3 us (50%)
  starting transfers between devices  32.5 us (31%)
  waiting for transfers between devices  11 us (10%)
  Pallas kernels  5.81 us (5%)
  other arithmetic  1.63 us (2%)
  between operations  1.39 us (1%)
    all_to_all x1, blocking collectives, per_device(): landed = lax.all_to_all(sent, BLOCK, 0, 0, tiled=True)  19.5 us
    all_to_all x1, blocking collectives, per_device(): fetched = lax.all_to_all(found, BLOCK, 0, 0, tiled=True)  18.6 us
    all_to_all x1, blocking collectives, per_device(): lax.all_to_all(copies.reshape(8, 16, WIDTH), ('core', 'rep'), 0, 0, tiled...  15.2 us
    ppermute x1, starting transfers between devices, per_device(): held = lax.ppermute(pair, RING, [(d, s) for s, d in spread_pairs()])  9.97 us
    ppermute x1, starting transfers between devices, per_device(): lax.ppermute(amplitudes, 'core', ((0, 1), (1, 0)))  8.77 us
    ppermute x1, starting transfers between devices, per_device(): back = lax.ppermute(part, RING, return_pairs())  8.21 us
    all_to_all x1, waiting for transfers between devices, per_device(): lax.all_to_all(want.reshape(PEERS, 1, 8), BLOCK, 0, 0, tiled=True)  7.39 us
    pallas_call x4, Pallas kernels, call(): pl.pallas_call(kernel, out_shape=shapes, in_specs=list(ins), out_specs=tu...  5.81 us
  transfers between devices with their start and end apart: 4, of which 2 were waited for; matrix products, arithmetic and copies ran while one was open for 0% of the time, Pallas kernels for 2%

profile of v6, /device:TPU:1, one launch (start us, length us, event | category | flops | bytes accessed | tf_op | source)
XLA Modules:
  0.0 105.7 jit_solution(3104583515240990126)
XLA Ops:
  0.6 0.9 convert.11
  1.5 8.8 %collective-permute-start = (bf16[16,1440]{1,0:T(8,128)(2,1)S(1)}, bf16[16,1440]{1,0:T(8,128)(2,1)S(1)}, u32[]{:S(2)}, u32[]{:S(2)}) collective-permute-start(bf16[16,1440]{1,0:T(8,128)(2,1)S(1)} %convert.11), channel_id=1, source_target_pairs={{0,4},{4,0},{1,5},{5,1},{2,6},{6,2},{3,7},{7,3},{8,12},{12,8},{9,1... | collective-permute-start | bytes 138248 | tf_op jit(solution)/shard_map/ppermute | solution.py:166
  11.0 1.6 %shard_map.95 = (s32[64,8]{1,0:T(8,128)}, s32[8,128]{1,0:T(8,128)S(1)}) custom-call(s32[1]{0:T(128)S(6)} %copy.12.count_ref, s32[1,128]{1,0:T(1,128)} %bitcast.16, s32[1,128]{1,0:T(1,128)} %bitcast.17, s32[1,128]{1,0:T(1,128)} %bitcast.18, s32[1,128]{1,0:T(1,128)} %bitcast.19), custom_call_target="tpu_custom_call" | custom-call | tf_op jit(solution)/shard_map/pallas_call | solution.py:127
  12.6 0.0 collective-permute-done
  12.6 10.0 %collective-permute-start.1 = (bf16[32,1440]{1,0:T(8,128)(2,1)S(1)}, bf16[32,1440]{1,0:T(8,128)(2,1)S(1)}, u32[]{:S(2)}, u32[]{:S(2)}) collective-permute-start(bf16[32,1440]{1,0:T(8,128)(2,1)S(1)} %pad_maximum_fusion), channel_id=1, source_target_pairs={{0,0},{17,1},{34,2},{51,3},{64,4},{81,5},{98,6},{115,7},{1,16},{16... | collective-permute-start | bytes 276488 | tf_op jit(solution)/shard_map/ppermute | solution.py:180
  22.6 5.5 %all-to-all-start = ((s32[64,1,8]{2,1,0:T(1,128)}), s32[64,1,8]{2,1,0:T(1,128)S(1)}, u32[]{:S(2)}, u32[]{:S(2)}) async-start(s32[64,1,8]{2,1,0:T(1,128)} %bitcast.15), calls=%async_computation | async-start | bytes 65536 | tf_op jit(solution)/shard_map/all_to_all | solution.py:181
  28.2 7.4 %all-to-all-done = s32[64,1,8]{2,1,0:T(1,128)S(1)} async-done(((s32[64,1,8]{2,1,0:T(1,128)}), s32[64,1,8]{2,1,0:T(1,128)S(1)}, u32[]{:S(2)}, u32[]{:S(2)}) %all-to-all-start) | async-done | bytes 2080 | tf_op jit(solution)/shard_map/all_to_all | solution.py:181
  35.6 0.0 collective-permute-done.1.rows_ref
  35.6 0.5 shard_map.96
  36.1 18.6 %all_to_all.20.rows_ref = bf16[64,4,1440]{2,1,0:T(4,128)(2,1)S(1)} all-to-all(bf16[64,4,1440]{2,1,0:T(4,128)(2,1)S(1)} %get-tuple-element.13), channel_id=1, replica_groups=mesh['x'=4,'zh'=8,'zl'=2,'core'=2,'rep'=4] {'core','x','zl','rep'}, dimensions={0} | all-to-all | bytes 1474560 | tf_op jit(solution)/shard_map/all_to_all | solution.py:192
  54.7 0.0 copy-start
  54.7 0.0 copy-start.2
  54.7 3.1 %shard_map.97 = bf16[64,4,1440]{2,1,0:T(4,128)(2,1)S(1)} custom-call(s32[8,128]{1,0:T(8,128)S(1)} %get-tuple-element.12.place_ref, bf16[64,4,1440]{2,1,0:T(4,128)(2,1)S(1)} %all_to_all.20.rows_ref, bf16[1440,1440]{1,0:T(8,128)(2,1)} %tile_hbm.1), custom_call_target="tpu_custom_call" | custom-call | tf_op jit(solution)/shard_map/pallas_call | solution.py:127
  57.8 19.5 %all_to_all.21.rows_ref = bf16[64,4,1440]{2,1,0:T(4,128)(2,1)S(1)} all-to-all(bf16[64,4,1440]{2,1,0:T(4,128)(2,1)S(1)} %shard_map.97), channel_id=1, replica_groups=mesh['x'=4,'zh'=8,'zl'=2,'core'=2,'rep'=4] {'core','x','zl','rep'}, dimensions={0} | all-to-all | bytes 1474560 | tf_op jit(solution)/shard_map/all_to_all | solution.py:203
  77.3 0.5 shard_map.98
  77.8 8.2 %collective-permute-start.2 = (bf16[32,1440]{1,0:T(8,128)(2,1)S(1)}, bf16[32,1440]{1,0:T(8,128)(2,1)S(1)}, u32[]{:S(2)}, u32[]{:S(2)}) collective-permute-start(bf16[32,1440]{1,0:T(8,128)(2,1)S(1)} %shard_map.98), channel_id=1, source_target_pairs={{0,2},{1,23},{2,33},{3,48},{4,64},{5,85},{6,103},{7,118},{16,7},{1... | collective-permute-start | bytes 276488 | tf_op jit(solution)/shard_map/ppermute | solution.py:212
  86.1 3.6 %collective-permute-done.2 = bf16[32,1440]{1,0:T(8,128)(2,1)S(1)} collective-permute-done((bf16[32,1440]{1,0:T(8,128)(2,1)S(1)}, bf16[32,1440]{1,0:T(8,128)(2,1)S(1)}, u32[]{:S(2)}, u32[]{:S(2)}) %collective-permute-start.2) | collective-permute-done | bytes 92192 | tf_op jit(solution)/shard_map/ppermute | solution.py:212
  89.7 15.2 %all_to_all.22 = bf16[8,16,1440]{2,1,0:T(8,128)(2,1)S(1)} all-to-all(bf16[8,16,1440]{2,1,0:T(8,128)(2,1)S(1)} %bitcast.13), channel_id=1, replica_groups=mesh['x'=4,'zh'=8,'zl'=2,'core'=2,'rep'=4] {'core','rep'}, dimensions={0} | all-to-all | bytes 737280 | tf_op jit(solution)/shard_map/all_to_all | solution.py:214
  104.9 0.1 convert_reduce_fusion
  105.0 0.0 copy-done
  105.0 0.0 copy-done.2
  105.0 0.0 copy-start.1
  105.0 0.7 divide_add_fusion
  105.7 0.0 copy-done.1
  (2 shorter events, 0.0 us)
Async XLA Ops:
  1.5 11.1 %collective-permute-start = (bf16[16,1440]{1,0:T(8,128)(2,1)S(1)}, bf16[16,1440]{1,0:T(8,128)(2,1)S(1)}, u32[]{:S(2)}, u32[]{:S(2)}) collective-permute-start(bf16[16,1440]{1,0:T(8,128)(2,1)S(1)} %convert.11), channel_id=1, source_target_pairs={{0,4},{4,0},{1,5},{5,1},{2,6},{6,2},{3,7},{7,3},{8,12},{12,8},{9,1... | collective-permute-start | bytes 138248 | tf_op jit(solution)/shard_map/ppermute | solution.py:166
  12.6 22.9 %collective-permute-start.1 = (bf16[32,1440]{1,0:T(8,128)(2,1)S(1)}, bf16[32,1440]{1,0:T(8,128)(2,1)S(1)}, u32[]{:S(2)}, u32[]{:S(2)}) collective-permute-start(bf16[32,1440]{1,0:T(8,128)(2,1)S(1)} %pad_maximum_fusion), channel_id=1, source_target_pairs={{0,0},{17,1},{34,2},{51,3},{64,4},{81,5},{98,6},{115,7},{1,16},{16... | collective-permute-start | bytes 276488 | tf_op jit(solution)/shard_map/ppermute | solution.py:180
  22.6 13.0 %all-to-all-start = ((s32[64,1,8]{2,1,0:T(1,128)}), s32[64,1,8]{2,1,0:T(1,128)S(1)}, u32[]{:S(2)}, u32[]{:S(2)}) async-start(s32[64,1,8]{2,1,0:T(1,128)} %bitcast.15), calls=%async_computation | async-start | bytes 65536 | tf_op jit(solution)/shard_map/all_to_all | solution.py:181
  54.7 50.3 %copy-start = (f32[16,1440]{1,0:T(8,128)S(1)}, f32[16,1440]{1,0:T(8,128)}, u32[]{:S(2)}) copy-start(f32[16,1440]{1,0:T(8,128)} %param.8) | copy-start | bytes 276484
  54.7 50.3 %copy-start.2 = (f32[16,1440]{1,0:T(8,128)S(1)}, f32[16,1440]{1,0:T(8,128)}, u32[]{:S(2)}) copy-start(f32[16,1440]{1,0:T(8,128)} %param.9) | copy-start | bytes 276484
  77.8 11.9 %collective-permute-start.2 = (bf16[32,1440]{1,0:T(8,128)(2,1)S(1)}, bf16[32,1440]{1,0:T(8,128)(2,1)S(1)}, u32[]{:S(2)}, u32[]{:S(2)}) collective-permute-start(bf16[32,1440]{1,0:T(8,128)(2,1)S(1)} %shard_map.98), channel_id=1, source_target_pairs={{0,2},{1,23},{2,33},{3,48},{4,64},{5,85},{6,103},{7,118},{16,7},{1... | collective-permute-start | bytes 276488 | tf_op jit(solution)/shard_map/ppermute | solution.py:212
  105.0 0.7 copy-start.1
